TPU v7x, 32 devices: a whole 2x2x4 slice. The times are simulated.
32 devices in a mesh: groups: 2 (over y), space: 4 (over z), tm: 4 (over x, core).
Axes of the slice: x: 2, y: 2, z: 4, core: 2. Of those that a mesh axis runs over, the one named last changes fastest.
Arguments:
- state: float32 [8, 4, 256, 256], P(('groups', 'tm'), 'space'), parts along dimension 0, may hold values from 0 to 1
- classes: int32 [8, 256, 256], P(('groups', 'space')), parts along dimension 0, may hold values from 0 to 3
- perm_table: float32 [4], replicated, may hold values from 0.2 to 2
- rate_table: float32 [4], replicated, may hold values from 0.02 to 1
Outputs:
- new_state: float32 [8, 4, 256, 256], P(('groups', 'tm'), 'space'), parts along dimension 0
There are 2 independent parts, one for each index of `groups`. A program takes and returns all parts, laid end to end along the dimension named above; an argument that names none is the same for every part. Nothing has to cross between parts.
All inputs are finite; a program needn't handle non-finite values.
Results may differ from a plain program's by a relative error of at most 0.0001.
Values sent between devices are 32-bit elements; how exact they have to be, the bound alone decides.
A program may use at most 64 MiB of HBM per device.

v0:
```python
import jax
import jax.numpy as jnp
from jax import lax
from jax.sharding import PartitionSpec as P

ITERS = 3
FINE = 2


DIFF = 2.0
ADV = 0.25


def with_halo(array, sides, width):
    for axis, dim in sides:
        devices, length = (lax.axis_size(axis), array.shape[dim])
        up = [(i, (i + 1) % devices) for i in range(devices)]
        down = [(j, i) for i, j in up]
        last = lax.slice_in_dim(array, length - width, length, axis=dim)
        first = lax.slice_in_dim(array, 0, width, axis=dim)
        before = lax.ppermute(last, axis, up)
        after = lax.ppermute(first, axis, down)
        array = jnp.concatenate([before, array, after], axis=dim)
    return array


def passed_along(array, axis, by):
    devices = lax.axis_size(axis)
    pairs = [(i, i + by) for i in range(devices) if 0 <= i + by < devices]
    return lax.ppermute(array, axis, pairs)


def lookup(table, classes):
    values = jnp.zeros(classes.shape, jnp.float32)
    for entry in range(table.shape[0]):
        values = jnp.where(classes == entry, table[entry], values)
    return values


def restrict(field):
    cx, ny, nz = field.shape
    return field.reshape(cx, ny // 2, 2, nz // 2, 2).mean(axis=(2, 4))


def prolong(coarse):
    return jnp.repeat(jnp.repeat(coarse, 2, axis=1), 2, axis=2)


def vertical(field):
    zero_plane = jnp.zeros(field.shape[:2] + (1,), jnp.float32)
    upper = jnp.concatenate([field[:, :, 1:], zero_plane], axis=2)
    lower = jnp.concatenate([zero_plane, field[:, :, :-1]], axis=2)
    return (upper, lower)


def operate(field):
    padded = with_halo(field, (("space", 0),), 1)
    upper, lower = vertical(field)
    beside = padded[2:] + padded[:-2]
    beside = beside + jnp.roll(field, -1, 1) + jnp.roll(field, 1, 1)
    beside = beside + upper + lower
    return (1.0 + 6.0 * DIFF) * field - DIFF * beside


def squares(residual):
    return lax.psum(jnp.sum(residual * residual), "space")


def fine_step(field, perm):
    upper, lower = vertical(field)
    rhs = field - ADV * perm * field * (upper - lower)
    solution = field
    residual = rhs - operate(solution)
    direction = residual
    norm_now = squares(residual)
    for step in range(ITERS):
        image = operate(direction)
        alpha = norm_now / lax.psum(jnp.sum(direction * image), "space")
        solution = solution + alpha * direction
        residual = residual - alpha * image
        norm_next = squares(residual)
        direction = residual + norm_next / norm_now * direction
        norm_now = norm_next
    return solution


def body(state, classes, perm_table, rate_table):
    start = state[0]
    perm = lookup(perm_table, classes)
    coarse_ratio = 1.0 / (1.0 + restrict(lookup(rate_table, classes)))
    field = start
    for step in range(FINE):
        field = fine_step(field, perm)
    coarse_start = restrict(start)
    jump = field - prolong(coarse_ratio * coarse_start)
    jump_coarse = restrict(jump)
    first = lax.axis_index("tm") == 0
    factor = jnp.where(first, 0.0, coarse_ratio)
    offset = jnp.where(first, coarse_ratio * coarse_start + jump_coarse, jump_coarse)
    before = passed_along(jump, "tm", 1)
    before_coarse = restrict(before)

    def relay_turn(turn, carry):
        outgoing, received = carry
        received = passed_along(outgoing, "tm", 1)
        return (factor * received + offset, received)

    outgoing, received = lax.fori_loop(
        0, lax.axis_size("tm") - 1, relay_turn, (offset, jnp.zeros_like(offset))
    )
    updated = jnp.where(first, start, before + prolong(received - before_coarse))
    return updated[None]


def solution(mesh):
    placed = (
        P(("groups", "tm"), "space", None, None),
        P(("groups", "space"), None, None),
        P(),
        P(),
    )
    return jax.shard_map(
        body,
        mesh=mesh,
        in_specs=placed,
        out_specs=P(("groups", "tm"), "space", None, None),
        check_vma=False,
    )
```

profile of v0, /device:TPU:3, one launch (start us, length us, event | category | flops | bytes accessed | tf_op | source)
XLA Modules:
  0.0 335.7 jit_solution(15333414936486038622)
XLA Ops:
  0.0 1.1 copy.16
  1.1 3.4 %collective-permute-start.1 = (f32[1,256,256]{1,2,0:T(8,128)S(1)}, f32[1,256,256]{1,2,0:T(8,128)S(1)}, u32[]{:S(2)}, u32[]{:S(2)}) collective-permute-start(f32[1,256,256]{1,2,0:T(8,128)S(1)} %bitcast.34), channel_id=1, source_target_pairs={{4,0},{8,4},{12,8},{0,12},{5,1},{9,5},{13,9},{1,13},{6,2},{10,6},{... | collective-permute-start | bytes 786440 | tf_op jit(solution)/shard_map/ppermute | solution.py:22
  4.7 1.5 fusion.76
  6.2 1.5 fusion.75
  7.7 18.9 %reshape_squeeze.3 = f32[128,2,128,2]{3,2,1,0:T(8,128)} reshape(f32[1,1,256,256]{3,2,1,0:T(8,128)} %param.6) | data formatting | bytes 524288 | tf_op jit(solution)/shard_map/reshape;squeeze | solution.py:42
  26.7 8.0 %reduce_sum.157 = f32[128,128]{1,0:T(8,128)S(1)} reduce(f32[128,2,128,2]{3,2,1,0:T(8,128)} %reshape_squeeze.3, f32[]{:T(128)} %constant.6.clone.1), dimensions={1,3}, to_apply=%region_25.26 | reduce | flops 49152 | bytes 327684 | tf_op jit(solution)/shard_map/reduce_sum | solution.py:42
  34.8 2.9 fusion.5
  37.7 3.3 collective-permute-start.3
  41.1 2.6 select_select_fusion
  43.9 18.1 %reshape.122 = f32[128,2,128,2]{3,2,1,0:T(8,128)} reshape(f32[1,256,256]{2,1,0:T(8,128)S(1)} %copy.21) | data formatting | bytes 524288 | tf_op jit(solution)/shard_map/reshape | solution.py:42
  62.1 0.9 multiply_reduce_fusion.8
  63.0 10.5 %all-reduce.17 = (f32[]{:T(128)}, f32[]{:T(128)}) all-reduce(f32[]{:T(128)} %get-tuple-element.35, f32[]{:T(128)} %get-tuple-element.34), channel_id=1, replica_groups=mesh['groups'=2,'space'=4,'tm'=4] {'space'}, use_global_device_ids=true, to_apply=%region_1.2 | all-reduce | flops 2 | bytes 16 | tf_op jit(solution)/shard_map/psum | solution.py:66
  74.8 0.7 multiply_reduce_fusion.7
  75.5 7.2 %psum.86 = f32[]{:T(128)} all-reduce(f32[]{:T(128)} %get-tuple-element.57), channel_id=1, replica_groups=mesh['groups'=2,'space'=4,'tm'=4] {'space'}, use_global_device_ids=true, to_apply=%region_5.6 | all-reduce | flops 1 | bytes 8 | tf_op jit(solution)/shard_map/psum | solution.py:66
  84.1 1.5 collective-permute-start.5
  85.9 3.5 %collective-permute-done.5 = f32[1,256,256]{1,2,0:T(8,128)S(1)} collective-permute-done((f32[1,256,256]{1,2,0:T(8,128)S(1)}, f32[1,256,256]{1,2,0:T(8,128)S(1)}, u32[]{:S(2)}, u32[]{:S(2)}) %collective-permute-start.5) | collective-permute-done | bytes 262176 | tf_op jit(solution)/shard_map/ppermute | solution.py:22
  89.4 3.3 collective-permute-done.6
  92.7 0.8 multiply_reduce_fusion.6
  93.6 9.3 %psum.87 = f32[]{:T(128)} all-reduce(f32[]{:T(128)} %get-tuple-element.55), channel_id=1, replica_groups=mesh['groups'=2,'space'=4,'tm'=4] {'space'}, use_global_device_ids=true, to_apply=%region_7.8 | all-reduce | flops 1 | bytes 8 | tf_op jit(solution)/shard_map/psum | solution.py:78
  104.2 0.7 multiply_reduce_fusion.5
  104.9 8.0 %reduce_sum.156 = f32[128,128]{1,0:T(8,128)S(1)} reduce(f32[128,2,128,2]{3,2,1,0:T(8,128)} %reshape.122, f32[]{:T(128)} %constant.6.clone.1), dimensions={1,3}, to_apply=%region_24.25 | reduce | flops 49152 | bytes 327684 | tf_op jit(solution)/shard_map/reduce_sum | solution.py:42
  112.9 7.2 %psum.88 = f32[]{:T(128)} all-reduce(f32[]{:T(128)} %multiply_reduce_fusion.5), channel_id=1, replica_groups=mesh['groups'=2,'space'=4,'tm'=4] {'space'}, use_global_device_ids=true, to_apply=%region_9.10 | all-reduce | flops 1 | bytes 8 | tf_op jit(solution)/shard_map/psum | solution.py:66
  121.5 1.5 collective-permute-start.7
  123.2 3.6 %collective-permute-done.7 = f32[1,256,256]{1,2,0:T(8,128)S(1)} collective-permute-done((f32[1,256,256]{1,2,0:T(8,128)S(1)}, f32[1,256,256]{1,2,0:T(8,128)S(1)}, u32[]{:S(2)}, u32[]{:S(2)}) %collective-permute-start.7) | collective-permute-done | bytes 262176 | tf_op jit(solution)/shard_map/ppermute | solution.py:22
  126.8 3.4 %collective-permute-done.8 = f32[1,256,256]{1,2,0:T(8,128)S(1)} collective-permute-done((f32[1,256,256]{1,2,0:T(8,128)S(1)}, f32[1,256,256]{1,2,0:T(8,128)S(1)}, u32[]{:S(2)}, u32[]{:S(2)}) %collective-permute-start.8) | collective-permute-done | bytes 262176 | tf_op jit(solution)/shard_map/ppermute | solution.py:21
  130.2 0.8 fusion.22
  131.1 9.0 %psum.89 = f32[]{:T(128)} all-reduce(f32[]{:T(128)} %fusion.22), channel_id=1, replica_groups=mesh['groups'=2,'space'=4,'tm'=4] {'space'}, use_global_device_ids=true, to_apply=%region_11.12 | all-reduce | flops 1 | bytes 8 | tf_op jit(solution)/shard_map/psum | solution.py:78
  142.0 1.1 collective-permute-start.10
  143.2 6.8 %collective-permute-done.9 = f32[1,256,256]{1,2,0:T(8,128)S(1)} collective-permute-done((f32[1,256,256]{1,2,0:T(8,128)S(1)}, f32[1,256,256]{1,2,0:T(8,128)S(1)}, u32[]{:S(2)}, u32[]{:S(2)}) %collective-permute-start.9) | collective-permute-done | bytes 262176 | tf_op jit(solution)/shard_map/ppermute | solution.py:22
  150.0 2.9 fusion.28
  152.9 0.8 collective-permute-start.11
  153.8 0.7 collective-permute-start.12
  154.7 3.5 %collective-permute-done.11 = f32[1,256,256]{1,2,0:T(8,128)S(1)} collective-permute-done((f32[1,256,256]{1,2,0:T(8,128)S(1)}, f32[1,256,256]{1,2,0:T(8,128)S(1)}, u32[]{:S(2)}, u32[]{:S(2)}) %collective-permute-start.11) | collective-permute-done | bytes 262176 | tf_op jit(solution)/shard_map/ppermute | solution.py:22
  158.2 7.6 %collective-permute-done.12 = f32[1,256,256]{1,2,0:T(8,128)S(1)} collective-permute-done((f32[1,256,256]{1,2,0:T(8,128)S(1)}, f32[1,256,256]{1,2,0:T(8,128)S(1)}, u32[]{:S(2)}, u32[]{:S(2)}) %collective-permute-start.12) | collective-permute-done | bytes 262176 | tf_op jit(solution)/shard_map/ppermute | solution.py:21
  165.8 0.9 multiply_reduce_fusion.3
  166.7 10.2 %all-reduce.16 = (f32[]{:T(128)}, f32[]{:T(128)}) all-reduce(f32[]{:T(128)} %get-tuple-element.33, f32[]{:T(128)} %get-tuple-element.32), channel_id=1, replica_groups=mesh['groups'=2,'space'=4,'tm'=4] {'space'}, use_global_device_ids=true, to_apply=%region_13.14 | all-reduce | flops 2 | bytes 16 | tf_op jit(solution)/shard_map/psum | solution.py:66
  178.8 7.2 %psum.92 = f32[]{:T(128)} all-reduce(f32[]{:T(128)} %get-tuple-element.52), channel_id=1, replica_groups=mesh['groups'=2,'space'=4,'tm'=4] {'space'}, use_global_device_ids=true, to_apply=%region_17.18 | all-reduce | flops 1 | bytes 8 | tf_op jit(solution)/shard_map/psum | solution.py:66
  187.4 1.5 collective-permute-start.13
  189.1 3.6 %collective-permute-done.13 = f32[1,256,256]{1,2,0:T(8,128)S(1)} collective-permute-done((f32[1,256,256]{1,2,0:T(8,128)S(1)}, f32[1,256,256]{1,2,0:T(8,128)S(1)}, u32[]{:S(2)}, u32[]{:S(2)}) %collective-permute-start.13) | collective-permute-done | bytes 262176 | tf_op jit(solution)/shard_map/ppermute | solution.py:22
  192.7 3.3 collective-permute-done.14
  196.0 0.9 multiply_reduce_fusion.1
  196.9 9.0 %psum.93 = f32[]{:T(128)} all-reduce(f32[]{:T(128)} %get-tuple-element.50), channel_id=1, replica_groups=mesh['groups'=2,'space'=4,'tm'=4] {'space'}, use_global_device_ids=true, to_apply=%region_19.20 | all-reduce | flops 1 | bytes 8 | tf_op jit(solution)/shard_map/psum | solution.py:78
  207.1 0.7 multiply_reduce_fusion
  208.0 8.2 %psum.94 = f32[]{:T(128)} all-reduce(f32[]{:T(128)} %multiply_reduce_fusion), channel_id=1, replica_groups=mesh['groups'=2,'space'=4,'tm'=4] {'space'}, use_global_device_ids=true, to_apply=%region_21.22 | all-reduce | flops 1 | bytes 8 | tf_op jit(solution)/shard_map/psum | solution.py:66
  217.8 1.0 collective-permute-start.15
  219.4 3.7 %collective-permute-done.15 = f32[1,256,256]{1,2,0:T(8,128)S(1)} collective-permute-done((f32[1,256,256]{1,2,0:T(8,128)S(1)}, f32[1,256,256]{1,2,0:T(8,128)S(1)}, u32[]{:S(2)}, u32[]{:S(2)}) %collective-permute-start.15) | collective-permute-done | bytes 262176 | tf_op jit(solution)/shard_map/ppermute | solution.py:22
  223.1 3.6 %collective-permute-done.16 = f32[1,256,256]{1,2,0:T(8,128)S(1)} collective-permute-done((f32[1,256,256]{1,2,0:T(8,128)S(1)}, f32[1,256,256]{1,2,0:T(8,128)S(1)}, u32[]{:S(2)}, u32[]{:S(2)}) %collective-permute-start.16) | collective-permute-done | bytes 262176 | tf_op jit(solution)/shard_map/ppermute | solution.py:21
  226.7 0.8 fusion.45
  227.8 8.7 %psum.95 = f32[]{:T(128)} all-reduce(f32[]{:T(128)} %fusion.45), channel_id=1, replica_groups=mesh['groups'=2,'space'=4,'tm'=4] {'space'}, use_global_device_ids=true, to_apply=%region_23.24 | all-reduce | flops 1 | bytes 8 | tf_op jit(solution)/shard_map/psum | solution.py:78
  238.0 1.3 collective-permute-start.17
  239.4 18.1 %reshape.123 = f32[128,2,128,2]{3,2,1,0:T(8,128)} reshape(f32[1,256,256]{2,1,0:T(8,128)S(1)} %copy.23) | data formatting | bytes 524288 | tf_op jit(solution)/shard_map/reshape | solution.py:42
  257.5 8.0 %reduce_sum.158 = f32[128,128]{1,0:T(8,128)S(1)} reduce(f32[128,2,128,2]{3,2,1,0:T(8,128)} %reshape.123, f32[]{:T(128)} %constant.6.clone.1), dimensions={1,3}, to_apply=%region_26.27 | reduce | flops 49152 | bytes 327684 | tf_op jit(solution)/shard_map/reduce_sum | solution.py:42
  265.6 0.7 collective-permute-done.17
  266.4 18.1 %reshape.124 = f32[128,2,128,2]{3,2,1,0:T(8,128)} reshape(f32[1,256,256]{2,1,0:T(8,128)S(1)} %copy.24) | data formatting | bytes 524288 | tf_op jit(solution)/shard_map/reshape | solution.py:42
  284.5 8.0 %reduce_sum.159 = f32[128,128]{1,0:T(8,128)S(1)} reduce(f32[128,2,128,2]{3,2,1,0:T(8,128)} %reshape.124, f32[]{:T(128)} %constant.6.clone.1), dimensions={1,3}, to_apply=%region_29.30 | reduce | flops 49152 | bytes 327684 | tf_op jit(solution)/shard_map/reduce_sum | solution.py:42
  292.5 41.0 %while.12 = (s32[]{:T(128)}, f32[1,128,128]{2,1,0:T(8,128)S(1)}, f32[1,128,128]{2,1,0:T(8,128)}, f32[1,128,128]{2,1,0:T(8,128)S(1)}, f32[1,128,128]{2,1,0:T(8,128)S(1)}, /*index=5*/s32[]{:T(128)}) while((s32[]{:T(128)}, f32[1,128,128]{2,1,0:T(8,128)S(1)}, f32[1,128,128]{2,1,0:T(8,128)}, f32[1,128,128]{2,1,0:T(8,128)S(1)}, ...), condition=%wide.region_28.29_spmd, body=%wide.region_27.28_spmd.sunk | while | flops 32770 | bytes 786569 | solution.py:108
  292.5 1.3 collective-permute-start
  293.8 26.7 %collective-permute-done = f32[1,128,128]{2,1,0:T(8,128)S(1)} collective-permute-done((f32[1,128,128]{2,1,0:T(8,128)S(1)}, f32[1,128,128]{2,1,0:T(8,128)S(1)}, u32[]{:S(2)}, u32[]{:S(2)}) %collective-permute-start) | collective-permute-done | bytes 65568 | tf_op jit(solution)/shard_map/while/body/eval_jaxpr/ppermute | solution.py:30
  321.1 1.3 collective-permute-start
  322.4 4.3 %collective-permute-done = f32[1,128,128]{2,1,0:T(8,128)S(1)} collective-permute-done((f32[1,128,128]{2,1,0:T(8,128)S(1)}, f32[1,128,128]{2,1,0:T(8,128)S(1)}, u32[]{:S(2)}, u32[]{:S(2)}) %collective-permute-start) | collective-permute-done | bytes 65568 | tf_op jit(solution)/shard_map/while/body/eval_jaxpr/ppermute | solution.py:30
  327.3 1.3 collective-permute-start
  328.6 4.3 %collective-permute-done = f32[1,128,128]{2,1,0:T(8,128)S(1)} collective-permute-done((f32[1,128,128]{2,1,0:T(8,128)S(1)}, f32[1,128,128]{2,1,0:T(8,128)S(1)}, u32[]{:S(2)}, u32[]{:S(2)}) %collective-permute-start) | collective-permute-done | bytes 65568 | tf_op jit(solution)/shard_map/while/body/eval_jaxpr/ppermute | solution.py:30
  333.5 0.8 fusion.46
  334.8 0.8 copy.26
  (71 shorter events, 7.5 us)
Async XLA Ops:
  0.0 26.5 %copy-start.1 = (s32[1,256,256]{2,1,0:T(8,128)S(1)}, s32[1,256,256]{2,1,0:T(8,128)}, u32[]{:S(2)}) copy-start(s32[1,256,256]{2,1,0:T(8,128)} %param.7) | copy-start | bytes 786436
  1.1 33.6 %collective-permute-start.1 = (f32[1,256,256]{1,2,0:T(8,128)S(1)}, f32[1,256,256]{1,2,0:T(8,128)S(1)}, u32[]{:S(2)}, u32[]{:S(2)}) collective-permute-start(f32[1,256,256]{1,2,0:T(8,128)S(1)} %bitcast.34), channel_id=1, source_target_pairs={{4,0},{8,4},{12,8},{0,12},{5,1},{9,5},{13,9},{1,13},{6,2},{10,6},{... | collective-permute-start | bytes 786440 | tf_op jit(solution)/shard_map/ppermute | solution.py:22
  4.5 30.2 %collective-permute-start.2 = (f32[1,256,256]{1,2,0:T(8,128)S(1)}, f32[1,256,256]{1,2,0:T(8,128)S(1)}, u32[]{:S(2)}, u32[]{:S(2)}) collective-permute-start(f32[1,256,256]{1,2,0:T(8,128)S(1)} %bitcast.35), channel_id=1, source_target_pairs={{0,4},{4,8},{8,12},{12,0},{1,5},{5,9},{9,13},{13,1},{2,6},{6,10},{... | collective-permute-start | bytes 786440 | tf_op jit(solution)/shard_map/ppermute | solution.py:21
  37.7 24.4 %collective-permute-start.3 = (f32[1,256,256]{1,2,0:T(8,128)S(1)}, f32[1,256,256]{1,2,0:T(8,128)S(1)}, u32[]{:S(2)}, u32[]{:S(2)}) collective-permute-start(f32[1,256,256]{1,2,0:T(8,128)S(1)} %get-tuple-element.60), channel_id=1, source_target_pairs={{4,0},{8,4},{12,8},{0,12},{5,1},{9,5},{13,9},{1,13},{6,2},{10,6},{... | collective-permute-start | bytes 786440 | tf_op jit(solution)/shard_map/ppermute | solution.py:22
  41.1 21.1 %collective-permute-start.4 = (f32[1,256,256]{1,2,0:T(8,128)S(1)}, f32[1,256,256]{1,2,0:T(8,128)S(1)}, u32[]{:S(2)}, u32[]{:S(2)}) collective-permute-start(f32[1,256,256]{1,2,0:T(8,128)S(1)} %get-tuple-element.60), channel_id=1, source_target_pairs={{0,4},{4,8},{8,12},{12,0},{1,5},{5,9},{9,13},{13,1},{2,6},{6,10},{... | collective-permute-start | bytes 786440 | tf_op jit(solution)/shard_map/ppermute | solution.py:21
  84.1 5.3 %collective-permute-start.5 = (f32[1,256,256]{1,2,0:T(8,128)S(1)}, f32[1,256,256]{1,2,0:T(8,128)S(1)}, u32[]{:S(2)}, u32[]{:S(2)}) collective-permute-start(f32[1,256,256]{1,2,0:T(8,128)S(1)} %multiply_add_fusion.5), channel_id=1, source_target_pairs={{4,0},{8,4},{12,8},{0,12},{5,1},{9,5},{13,9},{1,13},{6,2},{10,6},{... | collective-permute-start | bytes 786440 | tf_op jit(solution)/shard_map/ppermute | solution.py:22
  85.6 7.1 %collective-permute-start.6 = (f32[1,256,256]{1,2,0:T(8,128)S(1)}, f32[1,256,256]{1,2,0:T(8,128)S(1)}, u32[]{:S(2)}, u32[]{:S(2)}) collective-permute-start(f32[1,256,256]{1,2,0:T(8,128)S(1)} %multiply_add_fusion.5), channel_id=1, source_target_pairs={{0,4},{4,8},{8,12},{12,0},{1,5},{5,9},{9,13},{13,1},{2,6},{6,10},{... | collective-permute-start | bytes 786440 | tf_op jit(solution)/shard_map/ppermute | solution.py:21
  121.5 5.3 %collective-permute-start.7 = (f32[1,256,256]{1,2,0:T(8,128)S(1)}, f32[1,256,256]{1,2,0:T(8,128)S(1)}, u32[]{:S(2)}, u32[]{:S(2)}) collective-permute-start(f32[1,256,256]{1,2,0:T(8,128)S(1)} %multiply_add_fusion.4), channel_id=1, source_target_pairs={{4,0},{8,4},{12,8},{0,12},{5,1},{9,5},{13,9},{1,13},{6,2},{10,6},{... | collective-permute-start | bytes 786440 | tf_op jit(solution)/shard_map/ppermute | solution.py:22
  123.0 7.2 %collective-permute-start.8 = (f32[1,256,256]{1,2,0:T(8,128)S(1)}, f32[1,256,256]{1,2,0:T(8,128)S(1)}, u32[]{:S(2)}, u32[]{:S(2)}) collective-permute-start(f32[1,256,256]{1,2,0:T(8,128)S(1)} %multiply_add_fusion.4), channel_id=1, source_target_pairs={{0,4},{4,8},{8,12},{12,0},{1,5},{5,9},{9,13},{13,1},{2,6},{6,10},{... | collective-permute-start | bytes 786440 | tf_op jit(solution)/shard_map/ppermute | solution.py:21
  141.6 8.4 %collective-permute-start.9 = (f32[1,256,256]{1,2,0:T(8,128)S(1)}, f32[1,256,256]{1,2,0:T(8,128)S(1)}, u32[]{:S(2)}, u32[]{:S(2)}) collective-permute-start(f32[1,256,256]{1,2,0:T(8,128)S(1)} %multiply_add_fusion.3), channel_id=1, source_target_pairs={{4,0},{8,4},{12,8},{0,12},{5,1},{9,5},{13,9},{1,13},{6,2},{10,6},{... | collective-permute-start | bytes 786440 | tf_op jit(solution)/shard_map/ppermute | solution.py:22
  142.0 8.0 %collective-permute-start.10 = (f32[1,256,256]{1,2,0:T(8,128)S(1)}, f32[1,256,256]{1,2,0:T(8,128)S(1)}, u32[]{:S(2)}, u32[]{:S(2)}) collective-permute-start(f32[1,256,256]{1,2,0:T(8,128)S(1)} %multiply_add_fusion.3), channel_id=1, source_target_pairs={{0,4},{4,8},{8,12},{12,0},{1,5},{5,9},{9,13},{13,1},{2,6},{6,10},{... | collective-permute-start | bytes 786440 | tf_op jit(solution)/shard_map/ppermute | solution.py:21
  152.9 5.3 %collective-permute-start.11 = (f32[1,256,256]{1,2,0:T(8,128)S(1)}, f32[1,256,256]{1,2,0:T(8,128)S(1)}, u32[]{:S(2)}, u32[]{:S(2)}) collective-permute-start(f32[1,256,256]{1,2,0:T(8,128)S(1)} %fusion.28), channel_id=1, source_target_pairs={{4,0},{8,4},{12,8},{0,12},{5,1},{9,5},{13,9},{1,13},{6,2},{10,6},{... | collective-permute-start | bytes 786440 | tf_op jit(solution)/shard_map/ppermute | solution.py:22
  153.8 12.1 %collective-permute-start.12 = (f32[1,256,256]{1,2,0:T(8,128)S(1)}, f32[1,256,256]{1,2,0:T(8,128)S(1)}, u32[]{:S(2)}, u32[]{:S(2)}) collective-permute-start(f32[1,256,256]{1,2,0:T(8,128)S(1)} %fusion.28), channel_id=1, source_target_pairs={{0,4},{4,8},{8,12},{12,0},{1,5},{5,9},{9,13},{13,1},{2,6},{6,10},{... | collective-permute-start | bytes 786440 | tf_op jit(solution)/shard_map/ppermute | solution.py:21
  187.4 5.3 %collective-permute-start.13 = (f32[1,256,256]{1,2,0:T(8,128)S(1)}, f32[1,256,256]{1,2,0:T(8,128)S(1)}, u32[]{:S(2)}, u32[]{:S(2)}) collective-permute-start(f32[1,256,256]{1,2,0:T(8,128)S(1)} %multiply_add_fusion.2), channel_id=1, source_target_pairs={{4,0},{8,4},{12,8},{0,12},{5,1},{9,5},{13,9},{1,13},{6,2},{10,6},{... | collective-permute-start | bytes 786440 | tf_op jit(solution)/shard_map/ppermute | solution.py:22
  188.9 7.1 %collective-permute-start.14 = (f32[1,256,256]{1,2,0:T(8,128)S(1)}, f32[1,256,256]{1,2,0:T(8,128)S(1)}, u32[]{:S(2)}, u32[]{:S(2)}) collective-permute-start(f32[1,256,256]{1,2,0:T(8,128)S(1)} %multiply_add_fusion.2), channel_id=1, source_target_pairs={{0,4},{4,8},{8,12},{12,0},{1,5},{5,9},{9,13},{13,1},{2,6},{6,10},{... | collective-permute-start | bytes 786440 | tf_op jit(solution)/shard_map/ppermute | solution.py:21
  217.8 5.4 %collective-permute-start.15 = (f32[1,256,256]{1,2,0:T(8,128)S(1)}, f32[1,256,256]{1,2,0:T(8,128)S(1)}, u32[]{:S(2)}, u32[]{:S(2)}) collective-permute-start(f32[1,256,256]{1,2,0:T(8,128)S(1)} %multiply_add_fusion.1), channel_id=1, source_target_pairs={{4,0},{8,4},{12,8},{0,12},{5,1},{9,5},{13,9},{1,13},{6,2},{10,6},{... | collective-permute-start | bytes 786440 | tf_op jit(solution)/shard_map/ppermute | solution.py:22
  218.7 8.0 %collective-permute-start.16 = (f32[1,256,256]{1,2,0:T(8,128)S(1)}, f32[1,256,256]{1,2,0:T(8,128)S(1)}, u32[]{:S(2)}, u32[]{:S(2)}) collective-permute-start(f32[1,256,256]{1,2,0:T(8,128)S(1)} %multiply_add_fusion.1), channel_id=1, source_target_pairs={{0,4},{4,8},{8,12},{12,0},{1,5},{5,9},{9,13},{13,1},{2,6},{6,10},{... | collective-permute-start | bytes 786440 | tf_op jit(solution)/shard_map/ppermute | solution.py:21
  238.0 28.3 %collective-permute-start.17 = (f32[1,256,256]{1,2,0:T(8,128)S(1)}, f32[1,256,256]{1,2,0:T(8,128)S(1)}, u32[]{:S(2)}, u32[]{:S(2)}) collective-permute-start(f32[1,256,256]{1,2,0:T(8,128)S(1)} %add_subtract_fusion), channel_id=1, source_target_pairs={{0,1},{1,2},{2,3},{4,5},{5,6},{6,7},{8,9},{9,10},{10,11},{12,13},{... | collective-permute-start | bytes 786440 | tf_op jit(solution)/shard_map/ppermute | solution.py:30
  292.5 28.0 %collective-permute-start = (f32[1,128,128]{2,1,0:T(8,128)S(1)}, f32[1,128,128]{2,1,0:T(8,128)S(1)}, u32[]{:S(2)}, u32[]{:S(2)}) collective-permute-start(f32[1,128,128]{2,1,0:T(8,128)S(1)} %get-tuple-element.159), channel_id=1, source_target_pairs={{0,1},{1,2},{2,3},{4,5},{5,6},{6,7},{8,9},{9,10},{10,11},{12,13},{... | collective-permute-start | bytes 196616 | tf_op jit(solution)/shard_map/while/body/eval_jaxpr/ppermute | solution.py:30
  320.4 0.6 copy-start
  321.1 5.6 %collective-permute-start = (f32[1,128,128]{2,1,0:T(8,128)S(1)}, f32[1,128,128]{2,1,0:T(8,128)S(1)}, u32[]{:S(2)}, u32[]{:S(2)}) collective-permute-start(f32[1,128,128]{2,1,0:T(8,128)S(1)} %get-tuple-element.159), channel_id=1, source_target_pairs={{0,1},{1,2},{2,3},{4,5},{5,6},{6,7},{8,9},{9,10},{10,11},{12,13},{... | collective-permute-start | bytes 196616 | tf_op jit(solution)/shard_map/while/body/eval_jaxpr/ppermute | solution.py:30
  326.6 0.6 copy-start
  327.3 5.6 %collective-permute-start = (f32[1,128,128]{2,1,0:T(8,128)S(1)}, f32[1,128,128]{2,1,0:T(8,128)S(1)}, u32[]{:S(2)}, u32[]{:S(2)}) collective-permute-start(f32[1,128,128]{2,1,0:T(8,128)S(1)} %get-tuple-element.159), channel_id=1, source_target_pairs={{0,1},{1,2},{2,3},{4,5},{5,6},{6,7},{8,9},{9,10},{10,11},{12,13},{... | collective-permute-start | bytes 196616 | tf_op jit(solution)/shard_map/while/body/eval_jaxpr/ppermute | solution.py:30
  332.9 0.6 copy-start
where the time goes:
time: 339 us; the launch traced here: 336 us
  blocking collectives  86.5 us (26%)
  local copies, waits for them, and re-layouts  83.3 us (25%)
  waiting for transfers between devices  81.8 us (24%)
  other arithmetic  49.6 us (15%)
  starting transfers between devices  21 us (6%)
  between operations  13.3 us (4%)
    reshape x3, local copies, waits for them, and re-layouts, restrict(): return field.reshape(cx, ny // 2, 2, nz // 2, 2).mean(axis=(2, 4))  54.3 us
    psum x6, blocking collectives, squares(): return lax.psum(jnp.sum(residual * residual), 'space')  50.5 us
    psum x4, blocking collectives, fine_step(): alpha = norm_now / lax.psum(jnp.sum(direction * image), 'space')  35.9 us
    ppermute x4, waiting for transfers between devices, passed_along(): return lax.ppermute(array, axis, pairs)  35.9 us
    reduce_sum x4, other arithmetic, restrict(): return field.reshape(cx, ny // 2, 2, nz // 2, 2).mean(axis=(2, 4))  32 us
    ppermute x8, waiting for transfers between devices, with_halo(): after = lax.ppermute(first, axis, down)  24.7 us
    ppermute x8, waiting for transfers between devices, with_halo(): before = lax.ppermute(last, axis, up)  21.2 us
    another operation x1, local copies, waits for them, and re-layouts, restrict(): return field.reshape(cx, ny // 2, 2, nz // 2, 2).mean(axis=(2, 4))  18.9 us
  transfers between devices with their start and end apart: 20, of which 15 were waited for; matrix products, arithmetic and copies ran while one was open for 23% of the time, Pallas kernels for 0%

commit v1 on v0

--- a/solution.py
+++ b/solution.py
@@ -1,6 +1,10 @@
+import functools
+
 import jax
 import jax.numpy as jnp
 from jax import lax
+from jax.experimental import pallas as pl
+from jax.experimental.pallas import tpu as pltpu
 from jax.sharding import PartitionSpec as P
 
 ITERS = 3
@@ -9,6 +13,377 @@
 
 DIFF = 2.0
 ADV = 0.25
+
+CENTRE = 1.0 + 6.0 * DIFF
+SCALE = 0.125
+BESIDE = DIFF / SCALE
+LOWEST = CENTRE - 6.0 * DIFF
+HIGHEST = CENTRE + 6.0 * DIFF
+HALO = 8
+MOMENTS = 2 * ITERS
+F32 = jnp.float32
+BF16 = jnp.bfloat16
+
+
+def pieces(value):
+    high = value.astype(BF16)
+    rest = value - high.astype(F32)
+    middle = rest.astype(BF16)
+    low = (rest - middle.astype(F32)).astype(BF16)
+    return high, middle, low
+
+
+def times(value, matrix):
+    a, b, c = pieces(value)
+    dot = functools.partial(jnp.dot, preferred_element_type=F32)
+    return dot(a, matrix) + (dot(b, matrix) + dot(c, matrix))
+
+
+def times_left(matrix, value):
+    a, b, c = pieces(value)
+    dot = functools.partial(jnp.dot, preferred_element_type=F32)
+    return dot(matrix, a) + (dot(matrix, b) + dot(matrix, c))
+
+
+def pairs(small, large, along, value):
+    i = lax.broadcasted_iota(jnp.int32, (small, large) if along else (large, small), 0 if along else 1)
+    j = lax.broadcasted_iota(jnp.int32, (small, large) if along else (large, small), 1 if along else 0)
+    off = j - 2 * i
+    return jnp.where((off == 0) | (off == 1), value, 0.0).astype(BF16)
+
+
+def restricted(field):
+    ny, nz = field.shape
+    narrow = times(field, pairs(nz // 2, nz, False, 0.5))
+    return times_left(pairs(ny // 2, ny, True, 0.5), narrow)
+
+
+def prolonged(coarse):
+    cy, cz = coarse.shape
+    right = pairs(cz, 2 * cz, True, 1.0)
+    left = pairs(cy, 2 * cy, False, 1.0)
+    dot = functools.partial(jnp.dot, preferred_element_type=F32)
+    total = None
+    for piece in pieces(coarse):
+        wide = dot(left, dot(piece, right).astype(BF16))
+        total = wide if total is None else total + wide
+    return total
+
+
+def looked_up(table_ref, classes):
+    values = jnp.full(classes.shape, table_ref[0], F32)
+    for entry in range(1, table_ref.shape[0]):
+        values = jnp.where(classes == entry, table_ref[entry], values)
+    return values
+
+
+def coefficients(moments):
+    def inner(a, b):
+        total = None
+        for i, x in enumerate(a):
+            for j, y in enumerate(b):
+                term = x * y * moments[i + j]
+                total = term if total is None else total + term
+        return total
+
+    one = jnp.ones_like(moments[0])
+    residual, direction, solution = [one], [one], []
+    norm_now = moments[0]
+    for step in range(ITERS):
+        image = [CENTRE * d for d in direction] + [0.0 * one]
+        for i, d in enumerate(direction):
+            image[i + 1] = image[i + 1] - BESIDE * d
+        alpha = norm_now / inner(direction, image)
+        alpha = jnp.clip(alpha, 1.0 / HIGHEST, 1.0 / LOWEST)
+        for i, d in enumerate(direction):
+            if i < len(solution):
+                solution[i] = solution[i] + alpha * d
+            else:
+                solution.append(alpha * d)
+        if step == ITERS - 1:
+            break
+        residual = residual + [0.0 * one]
+        residual = [r - alpha * a for r, a in zip(residual, image)]
+        norm_next = inner(residual, residual)
+        beta = jnp.clip(norm_next / norm_now, 0.0, HIGHEST - LOWEST)
+        direction = [r + beta * d for r, d in zip(residual, direction + [0.0 * one])]
+        norm_now = norm_next
+    return solution
+
+
+def kernel(S, T, state_ref, classes_ref, perm_ref, rate_ref, out_ref,
+           ext, extk, cbuf, kbuf, nbuf, dbuf, w0, w1, w2, w3, d0, d1, d2, perm_buf,
+           q_buf, msrc, mbuf, jsrc, jbuf, gsrc, gbuf, ssrc, sbuf,
+           local_sem, c_send, c_recv, k_send, k_recv, m_send, m_recv,
+           j_send, j_recv, g_send, g_recv, s_send, s_recv):
+    NY, NZ = state_ref.shape
+    rows = NY // S
+    slab = rows + 2 * HALO
+    own = slice(HALO, HALO + rows)
+    me = lax.axis_index("space")
+    t = lax.axis_index("tm")
+
+    local = []
+    for n, (source, target) in enumerate(((state_ref, ext), (classes_ref, extk))):
+        local += [
+            pltpu.make_async_copy(source, target.at[pl.ds(HALO, NY)], local_sem.at[3 * n]),
+            pltpu.make_async_copy(
+                source.at[pl.ds(NY - HALO, HALO)], target.at[pl.ds(0, HALO)], local_sem.at[3 * n + 1]),
+            pltpu.make_async_copy(
+                source.at[pl.ds(0, HALO)], target.at[pl.ds(HALO + NY, HALO)], local_sem.at[3 * n + 2]),
+        ]
+    for copy in local:
+        copy.start()
+
+    barrier = pltpu.get_barrier_semaphore()
+    for dt in range(T):
+        for dz in range(S):
+            if dt or dz:
+                pl.semaphore_signal(
+                    barrier, inc=1,
+                    device_id={"tm": lax.rem(t + dt, T), "space": lax.rem(me + dz, S)},
+                    device_id_type=pl.DeviceIdType.MESH)
+    for copy in local:
+        copy.wait()
+    pl.semaphore_wait(barrier, S * T - 1)
+
+    def slab_copy(source, target, send, recv, d):
+        to = lax.rem(me + d, S)
+        return pltpu.make_async_remote_copy(
+            src_ref=source.at[pl.ds(pl.multiple_of(to * rows, 8), slab)],
+            dst_ref=target.at[me],
+            send_sem=send.at[d - 1], recv_sem=recv.at[d - 1],
+            device_id={"space": to}, device_id_type=pl.DeviceIdType.MESH)
+
+    c_copies = [slab_copy(ext, cbuf, c_send, c_recv, d) for d in range(1, S)]
+    k_copies = [slab_copy(extk, kbuf, k_send, k_recv, d) for d in range(1, S)]
+    for copy in c_copies:
+        copy.start()
+    for copy in k_copies:
+        copy.start()
+    mine = pl.ds(pl.multiple_of(me * rows, 8), slab)
+    cbuf[me] = ext[mine]
+    kbuf[me] = extk[mine]
+
+    ssrc[...] = restricted(ext[HALO:HALO + NY])
+    s_copies = [
+        pltpu.make_async_remote_copy(
+            src_ref=ssrc, dst_ref=sbuf, send_sem=s_send.at[d - 1], recv_sem=s_recv.at[0],
+            device_id={"tm": lax.rem(t + d, T)}, device_id_type=pl.DeviceIdType.MESH)
+        for d in range(1, T)
+    ]
+
+    @pl.when(t == 0)
+    def _():
+        for copy in s_copies:
+            copy.start()
+
+    out_ratio = 1.0 / (1.0 + restricted(looked_up(rate_ref, extk[HALO:HALO + NY])))
+
+    i = lax.broadcasted_iota(jnp.int32, (NZ, NZ), 0)
+    j = lax.broadcasted_iota(jnp.int32, (NZ, NZ), 1)
+    up, down = i - j == 1, j - i == 1
+    both = jnp.where(up | down, 1.0, 0.0).astype(BF16)
+    apart = jnp.where(up, 1.0, jnp.where(down, -1.0, 0.0)).astype(BF16)
+
+    def neighbours(ref, p):
+        value = ref[p]
+        total = times(value, both)
+        total = total + (ref[(p + 1) % S] + ref[(p + S - 1) % S])
+        total = total + (pltpu.roll(value, 1, 0) + pltpu.roll(value, slab - 1, 0))
+        return SCALE * total
+
+    def dot_rows(a, b):
+        product = (a * b)[own]
+        return product.reshape(rows // 8, 8, NZ).sum(axis=0)
+
+    for copy in c_copies:
+        copy.wait_recv()
+    for p in range(S):
+        nbuf[p] = neighbours(cbuf, p)
+        dbuf[p] = times(cbuf[p], apart)
+    for copy in k_copies:
+        copy.wait_recv()
+    for p in range(S):
+        c = cbuf[p]
+        perm = looked_up(perm_ref, kbuf[p])
+        perm_buf[p] = perm
+        w0[p] = c - ADV * perm * c * dbuf[p] - CENTRE * c + BESIDE * nbuf[p]
+
+    krylov = (w0, w1, w2, w3)
+    for fine in range(FINE):
+        sums = [None] * MOMENTS
+        for k in range(ITERS):
+            source, target = krylov[k], krylov[k + 1]
+            for p in range(S):
+                value = neighbours(source, p)
+                target[p] = value
+                here = source[p]
+                for order, term in ((2 * k, dot_rows(here, here)), (2 * k + 1, dot_rows(here, value))):
+                    sums[order] = term if sums[order] is None else sums[order] + term
+        lines = [jnp.sum(s[:, :NZ // 2] + s[:, NZ // 2:], axis=0, keepdims=True) for s in sums]
+        lines = lines + [jnp.zeros_like(lines[0])] * (8 - MOMENTS)
+        msrc[fine] = jnp.concatenate(lines, axis=0)
+        mbuf[fine, me] = msrc[fine]
+        m_copies = [
+            pltpu.make_async_remote_copy(
+                src_ref=msrc.at[fine], dst_ref=mbuf.at[fine, me],
+                send_sem=m_send.at[fine, d - 1], recv_sem=m_recv.at[fine, d - 1],
+                device_id={"space": lax.rem(me + d, S)}, device_id_type=pl.DeviceIdType.MESH)
+            for d in range(1, S)
+        ]
+        for copy in m_copies:
+            copy.start()
+        if fine < FINE - 1:
+            for p in range(S):
+                d0[p] = times(w0[p], apart)
+                d1[p] = times(w1[p], apart)
+                d2[p] = times(w2[p], apart)
+        if fine == 0:
+            whole = jnp.concatenate([cbuf[p][own] for p in range(S)], axis=0)
+            kinds = jnp.concatenate([kbuf[p][own] for p in range(S)], axis=0)
+            ratio = 1.0 / (1.0 + restricted(looked_up(rate_ref, kinds)))
+            q_buf[...] = ratio * restricted(whole)
+        if fine == FINE - 1:
+            from_start = prolonged(q_buf[...])
+            for p in range(S):
+                jsrc[p] = cbuf[p][own] - from_start[p * rows:(p + 1) * rows]
+        for copy in m_copies:
+            copy.wait()
+        total = mbuf[fine, 0]
+        for d in range(1, S):
+            total = total + mbuf[fine, d]
+        total = jnp.sum(total, axis=1, keepdims=True)
+        found = [jnp.broadcast_to(total[k:k + 1, :], (1, NZ)) for k in range(MOMENTS)]
+        a = coefficients(found)
+        if fine < FINE - 1:
+            for p in range(S):
+                x0, x1, x2, x3 = w0[p], w1[p], w2[p], w3[p]
+                c = cbuf[p] + a[0] * x0 + a[1] * x1 + a[2] * x2
+                near = nbuf[p] + a[0] * x1 + a[1] * x2 + a[2] * x3
+                apart_c = dbuf[p] + a[0] * d0[p] + a[1] * d1[p] + a[2] * d2[p]
+                cbuf[p] = c
+                nbuf[p] = near
+                dbuf[p] = apart_c
+                w0[p] = c - ADV * perm_buf[p] * c * apart_c - CENTRE * c + BESIDE * near
+        else:
+            for p in range(S):
+                jsrc[p] += a[0] * w0[p][own] + a[1] * w1[p][own] + a[2] * w2[p][own]
+
+    def jump_copy(p):
+        return pltpu.make_async_remote_copy(
+            src_ref=jsrc.at[p], dst_ref=jbuf.at[me],
+            send_sem=j_send.at[p], recv_sem=j_recv.at[me],
+            device_id={"tm": lax.rem(t + 1, T), "space": p}, device_id_type=pl.DeviceIdType.MESH)
+
+    def coarse_copy(p, ahead):
+        return pltpu.make_async_remote_copy(
+            src_ref=gsrc.at[p], dst_ref=gbuf.at[lax.rem(t, T - 2), me],
+            send_sem=g_send.at[ahead - 2, p], recv_sem=g_recv.at[lax.rem(t, T - 2), me],
+            device_id={"tm": lax.rem(t + ahead, T), "space": p}, device_id_type=pl.DeviceIdType.MESH)
+
+    @pl.when(t < T - 1)
+    def _():
+        for p in range(S):
+            jump_copy(p).start()
+
+    @pl.when(t < T - 2)
+    def _():
+        jump = jsrc[...].reshape(NY, NZ)
+        gsrc[...] = restricted(jump).reshape(S, rows // 2, NZ // 2)
+        for ahead in range(2, T):
+            @pl.when(t + ahead < T)
+            def _():
+                for p in range(S):
+                    coarse_copy(p, ahead).start()
+
+    @pl.when(t == 0)
+    def _():
+        out_ref[...] = ext[HALO:HALO + NY]
+        for copy in s_copies:
+            copy.wait_send()
+
+    @pl.when(t > 0)
+    def _():
+        s_copies[0].wait_recv()
+        for k in range(T - 2):
+            @pl.when(k < t - 1)
+            def _():
+                for p in range(S):
+                    pltpu.make_async_remote_copy(
+                        src_ref=gsrc.at[p], dst_ref=gbuf.at[k, p],
+                        send_sem=g_send.at[0, p], recv_sem=g_recv.at[k, p],
+                        device_id={"tm": lax.rem(t + 1, T), "space": p},
+                        device_id_type=pl.DeviceIdType.MESH).wait_recv()
+                sbuf[...] = out_ratio * sbuf[...] + gbuf[k].reshape(NY // 2, NZ // 2)
+        wide = prolonged(out_ratio * sbuf[...])
+        for p in range(S):
+            pltpu.make_async_remote_copy(
+                src_ref=jsrc.at[p], dst_ref=jbuf.at[p],
+                send_sem=j_send.at[p], recv_sem=j_recv.at[p],
+                device_id={"tm": lax.rem(t + 1, T), "space": p},
+                device_id_type=pl.DeviceIdType.MESH).wait_recv()
+        out_ref[...] = wide + jbuf[...].reshape(NY, NZ)
+
+    for copy in c_copies:
+        copy.wait_send()
+    for copy in k_copies:
+        copy.wait_send()
+
+    @pl.when(t < T - 1)
+    def _():
+        for p in range(S):
+            jump_copy(p).wait_send()
+    for ahead in range(2, T):
+        @pl.when(t + ahead < T)
+        def _():
+            for p in range(S):
+                coarse_copy(p, ahead).wait_send()
+
+
+def fused_body(S, T, state, classes, perm_table, rate_table):
+    ny, nz = state.shape[2:]
+    rows = ny // S
+    slab = rows + 2 * HALO
+    field = pltpu.VMEM((S, slab, nz), F32)
+    dma = pltpu.SemaphoreType.DMA
+    updated = pl.pallas_call(
+        functools.partial(kernel, S, T),
+        out_shape=jax.ShapeDtypeStruct((ny, nz), F32),
+        in_specs=[
+            pl.BlockSpec(memory_space=pl.ANY),
+            pl.BlockSpec(memory_space=pl.ANY),
+            pl.BlockSpec(memory_space=pltpu.SMEM),
+            pl.BlockSpec(memory_space=pltpu.SMEM),
+        ],
+        out_specs=pl.BlockSpec(memory_space=pltpu.VMEM),
+        scratch_shapes=[
+            pltpu.VMEM((ny + 2 * HALO, nz), F32),
+            pltpu.VMEM((ny + 2 * HALO, nz), jnp.int32),
+            field,
+            pltpu.VMEM((S, slab, nz), jnp.int32),
+        ] + [field] * 10 + [
+            pltpu.VMEM((ny // 2, nz // 2), F32),
+            pltpu.VMEM((FINE, 8, nz // 2), F32),
+            pltpu.VMEM((FINE, S, 8, nz // 2), F32),
+            pltpu.VMEM((S, rows, nz), F32),
+            pltpu.VMEM((S, rows, nz), F32),
+            pltpu.VMEM((S, rows // 2, nz // 2), F32),
+            pltpu.VMEM((T - 2, S, rows // 2, nz // 2), F32),
+            pltpu.VMEM((ny // 2, nz // 2), F32),
+            pltpu.VMEM((ny // 2, nz // 2), F32),
+            dma((6,)),
+            dma((S - 1,)), dma((S - 1,)),
+            dma((S - 1,)), dma((S - 1,)),
+            dma((FINE, S - 1)), dma((FINE, S - 1)),
+            dma((S,)), dma((S,)),
+            dma((T - 2, S)), dma((T - 2, S)),
+            dma((T - 1,)), dma((1,)),
+        ],
+        compiler_params=pltpu.CompilerParams(
+            collective_id=0, has_side_effects=True, vmem_limit_bytes=40 * 1024 * 1024),
+    )(state[0, 0], classes[0], perm_table, rate_table)
+    return updated[None, None]
 
 
 def with_halo(array, sides, width):
@@ -119,8 +494,17 @@
         P(),
         P(),
     )
+    devices, slices = (mesh.shape["space"], mesh.shape["tm"])
+
+    def chosen(state, classes, perm_table, rate_table):
+        planes, ny, nz = state.shape[1:]
+        fits = planes == 1 and ny // devices >= 4 * HALO and nz % 256 == 0
+        if fits and slices >= 3 and devices >= 3:
+            return fused_body(devices, slices, state, classes, perm_table, rate_table)
+        return body(state, classes, perm_table, rate_table)
+
     return jax.shard_map(
-        body,
+        chosen,
         mesh=mesh,
         in_specs=placed,
         out_specs=P(("groups", "tm"), "space", None, None),

time: 339 us -> 43.8 us (0.13)
  blocking collectives: 86.5 us -> 0 us
  waiting for transfers between devices: 81.8 us -> 0 us
  local copies, waits for them, and re-layouts: 83.3 us -> 3.27 us
  other arithmetic: 49.6 us -> 0 us
  Pallas kernels: 0 us -> 40.3 us
  starting transfers between devices: 21 us -> 0 us
  between operations: 13.3 us -> 0.01 us
    psum x10 -> x0, blocking collectives: 86.5 us -> none  [the longest x6 50.5 us: squares(): return lax.psum(jnp.sum(residual * residual), 'space')]
    ppermute x20 -> x0, waiting for transfers between devices: 81.8 us -> none  [the longest x4 35.9 us: passed_along(): return lax.ppermute(array, axis, pairs)]
    reshape x3 -> x0, local copies, waits for them, and re-layouts: 54.3 us -> none  [restrict(): return field.reshape(cx, ny // 2, 2, nz // 2, 2).mean(axis=(2, 4))]
    pallas_call x0 -> x1, Pallas kernels: none -> 40.3 us  [fused_body(): pl.pallas_call(functools.partial(kernel, S, T), out_shape=jax.ShapeDtypeS...]
    reduce_sum x14 -> x0, other arithmetic: 39.9 us -> none  [the longest x4 32 us: restrict(): return field.reshape(cx, ny // 2, 2, nz // 2, 2).mean(axis=(2, 4))]
    ppermute x20 -> x0, starting transfers between devices: 21 us -> none  [the longest x8 13.4 us: with_halo(): after = lax.ppermute(first, axis, down)]
    another operation x1 -> x0, local copies, waits for them, and re-layouts: 18.9 us -> none  [restrict(): return field.reshape(cx, ny // 2, 2, nz // 2, 2).mean(axis=(2, 4))]
    sub x4 -> x0, other arithmetic: 6.74 us -> none  [the longest x2 5.81 us: fine_step(): residual = rhs - operate(solution)]
  transfers between devices with their start and end apart: 20 -> 0, of which waited for: 15 -> 0; matrix products, arithmetic and copies ran while one was open for 23% -> 0% of each run, Pallas kernels for 0% -> 0%
where the time goes in v1:
time: 43.8 us; the launch traced here: 43.6 us
  Pallas kernels  40.3 us (92%)
  local copies, waits for them, and re-layouts  3.27 us (7%)
    pallas_call x1, Pallas kernels, fused_body(): pl.pallas_call(functools.partial(kernel, S, T), out_shape=jax.ShapeDtypeS...  40.3 us
    unnamed x9, local copies, waits for them, and re-layouts  3.27 us

profile of v1, /device:TPU:3, one launch (start us, length us, event | category | flops | bytes accessed | tf_op | source)
XLA Modules:
  0.0 43.6 jit_solution(15420438269372936251)
XLA Ops:
  0.0 0.0 copy-start.2
  0.0 0.0 copy-start.3
  0.0 0.7 %copy-done.2 = f32[4]{0:T(128)S(1)} copy-done((f32[4]{0:T(128)S(1)}, f32[4]{0:T(128)}, u32[]{:S(2)}) %copy-start.2) | copy-done | bytes 40
  0.7 0.0 copy-done.3
  0.7 0.0 copy-start
  0.7 0.9 %copy-done = f32[1,1,256,256]{3,2,1,0:T(8,128)S(1)} copy-done((f32[1,1,256,256]{3,2,1,0:T(8,128)S(1)}, f32[1,1,256,256]{3,2,1,0:T(8,128)}, u32[]{:S(2)}) %copy-start) | copy-done | bytes 262168
  1.6 0.0 copy-start.1
  1.6 0.9 %copy-done.1 = s32[1,256,256]{2,1,0:T(8,128)S(1)} copy-done((s32[1,256,256]{2,1,0:T(8,128)S(1)}, s32[1,256,256]{2,1,0:T(8,128)}, u32[]{:S(2)}) %copy-start.1) | copy-done | bytes 262168
  2.6 40.3 %shard_map.46 = f32[256,256]{1,0:T(8,128)S(1)} custom-call(f32[256,256]{1,0:T(8,128)S(1)} %bitcast.4, s32[256,256]{1,0:T(8,128)S(1)} %bitcast.5, f32[4]{0:T(128)S(1)} %copy-done.2, f32[4]{0:T(128)S(1)} %copy-done.3), custom_call_target="tpu_custom_call" | custom-call | tf_op jit(solution)/shard_map/pallas_call | solution.py:350
  42.9 0.7 %copy.6 = f32[1,1,256,256]{3,2,1,0:T(8,128)} copy(f32[1,1,256,256]{3,2,1,0:T(8,128)S(1)} %bitcast.3) | data formatting | bytes 524288
Async XLA Ops:
  0.0 0.7 %copy-start.2 = (f32[4]{0:T(128)S(1)}, f32[4]{0:T(128)}, u32[]{:S(2)}) copy-start(f32[4]{0:T(128)} %perm_ref.1) | copy-start | bytes 52
  0.0 0.7 %copy-start.3 = (f32[4]{0:T(128)S(1)}, f32[4]{0:T(128)}, u32[]{:S(2)}) copy-start(f32[4]{0:T(128)} %rate_ref.1) | copy-start | bytes 52
  0.7 0.9 %copy-start = (f32[1,1,256,256]{3,2,1,0:T(8,128)S(1)}, f32[1,1,256,256]{3,2,1,0:T(8,128)}, u32[]{:S(2)}) copy-start(f32[1,1,256,256]{3,2,1,0:T(8,128)} %param.4) | copy-start | bytes 786436
  1.6 0.9 %copy-start.1 = (s32[1,256,256]{2,1,0:T(8,128)S(1)}, s32[1,256,256]{2,1,0:T(8,128)}, u32[]{:S(2)}) copy-start(s32[1,256,256]{2,1,0:T(8,128)} %param.5) | copy-start | bytes 786436

commit v2 on v1

--- a/solution.py
+++ b/solution.py
@@ -111,11 +111,11 @@
     return solution
 
 
-def kernel(S, T, state_ref, classes_ref, perm_ref, rate_ref, out_ref,
+def kernel(S, T, state_ref, classes_ref, perm_hbm, rate_hbm, out_ref,
            ext, extk, cbuf, kbuf, nbuf, dbuf, w0, w1, w2, w3, d0, d1, d2, perm_buf,
-           q_buf, msrc, mbuf, jsrc, jbuf, gsrc, gbuf, ssrc, sbuf,
-           local_sem, c_send, c_recv, k_send, k_recv, m_send, m_recv,
-           j_send, j_recv, g_send, g_recv, s_send, s_recv):
+           perm_ref, rate_ref, rs_buf, ratio_buf, msrc, mbuf, jsrc, jbuf, gsrc, gbuf, hsrc, hbuf,
+           local_sem, c_send, c_recv, k_send, k_recv, f_send, f_recv, m_send, m_recv,
+           j_send, j_recv, g_send, g_recv, h_send, h_recv):
     NY, NZ = state_ref.shape
     rows = NY // S
     slab = rows + 2 * HALO
@@ -132,53 +132,72 @@
             pltpu.make_async_copy(
                 source.at[pl.ds(0, HALO)], target.at[pl.ds(HALO + NY, HALO)], local_sem.at[3 * n + 2]),
         ]
+    local += [
+        pltpu.make_async_copy(perm_hbm, perm_ref, local_sem.at[6]),
+        pltpu.make_async_copy(rate_hbm, rate_ref, local_sem.at[7]),
+    ]
     for copy in local:
         copy.start()
 
     barrier = pltpu.get_barrier_semaphore()
-    for dt in range(T):
-        for dz in range(S):
-            if dt or dz:
-                pl.semaphore_signal(
-                    barrier, inc=1,
-                    device_id={"tm": lax.rem(t + dt, T), "space": lax.rem(me + dz, S)},
-                    device_id_type=pl.DeviceIdType.MESH)
+    partners = [(dt, dz) for dt in range(T) for dz in range(S) if dz == 0 or dt in (0, 1, T - 1)][1:]
+    for dt, dz in partners:
+        pl.semaphore_signal(
+            barrier, inc=1,
+            device_id={"tm": lax.rem(t + dt, T), "space": lax.rem(me + dz, S)},
+            device_id_type=pl.DeviceIdType.MESH)
     for copy in local:
         copy.wait()
-    pl.semaphore_wait(barrier, S * T - 1)
-
-    def slab_copy(source, target, send, recv, d):
+    pl.semaphore_wait(barrier, len(partners))
+
+    high, wide = slab // 2, NZ // 2
+    row_part, lane_part = lax.rem(t, 2), lax.div(t, 2)
+    lanes = pl.ds(pl.multiple_of(lane_part * wide, 128), wide)
+    quarter_rows = pl.ds(pl.multiple_of(row_part * high, 8), high)
+
+    def class_copy(d):
+        to = lax.rem(me + d, S)
+        start = pl.multiple_of(to * rows + row_part * high, 8)
+        return pltpu.make_async_remote_copy(
+            src_ref=extk.at[pl.ds(start, high), lanes],
+            dst_ref=kbuf.at[me, quarter_rows, lanes],
+            send_sem=k_send.at[d - 1], recv_sem=k_recv.at[d - 1],
+            device_id={"space": to}, device_id_type=pl.DeviceIdType.MESH)
+
+    def class_forward(d, e):
+        place = kbuf.at[lax.rem(me + S - d, S), quarter_rows, lanes]
+        return pltpu.make_async_remote_copy(
+            src_ref=place, dst_ref=place,
+            send_sem=f_send.at[d - 1, e - 1], recv_sem=f_recv.at[d - 1, e - 1],
+            device_id={"tm": lax.rem(t + e, T)}, device_id_type=pl.DeviceIdType.MESH)
+
+    def slab_copy(d):
         to = lax.rem(me + d, S)
         return pltpu.make_async_remote_copy(
-            src_ref=source.at[pl.ds(pl.multiple_of(to * rows, 8), slab)],
-            dst_ref=target.at[me],
-            send_sem=send.at[d - 1], recv_sem=recv.at[d - 1],
+            src_ref=ext.at[pl.ds(pl.multiple_of(to * rows, 8), slab)],
+            dst_ref=cbuf.at[me],
+            send_sem=c_send.at[d - 1], recv_sem=c_recv.at[d - 1],
             device_id={"space": to}, device_id_type=pl.DeviceIdType.MESH)
 
-    c_copies = [slab_copy(ext, cbuf, c_send, c_recv, d) for d in range(1, S)]
-    k_copies = [slab_copy(extk, kbuf, k_send, k_recv, d) for d in range(1, S)]
+    k_copies = [class_copy(d) for d in range(1, S)]
+    c_copies = [slab_copy(d) for d in range(1, S)]
+    f_copies = [class_forward(d, e) for d in range(1, S) for e in range(1, T)]
+    for copy in k_copies:
+        copy.start()
     for copy in c_copies:
-        copy.start()
-    for copy in k_copies:
         copy.start()
     mine = pl.ds(pl.multiple_of(me * rows, 8), slab)
     cbuf[me] = ext[mine]
     kbuf[me] = extk[mine]
 
-    ssrc[...] = restricted(ext[HALO:HALO + NY])
-    s_copies = [
-        pltpu.make_async_remote_copy(
-            src_ref=ssrc, dst_ref=sbuf, send_sem=s_send.at[d - 1], recv_sem=s_recv.at[0],
-            device_id={"tm": lax.rem(t + d, T)}, device_id_type=pl.DeviceIdType.MESH)
-        for d in range(1, T)
-    ]
-
     @pl.when(t == 0)
     def _():
-        for copy in s_copies:
-            copy.start()
-
-    out_ratio = 1.0 / (1.0 + restricted(looked_up(rate_ref, extk[HALO:HALO + NY])))
+        out_ref[...] = ext[HALO:HALO + NY]
+
+    for d in range(1, S):
+        k_copies[d - 1].wait_recv()
+        for e in range(1, T):
+            f_copies[(d - 1) * (T - 1) + e - 1].start()
 
     i = lax.broadcasted_iota(jnp.int32, (NZ, NZ), 0)
     j = lax.broadcasted_iota(jnp.int32, (NZ, NZ), 1)
@@ -202,13 +221,26 @@
     for p in range(S):
         nbuf[p] = neighbours(cbuf, p)
         dbuf[p] = times(cbuf[p], apart)
-    for copy in k_copies:
+    for copy in f_copies:
         copy.wait_recv()
     for p in range(S):
         c = cbuf[p]
         perm = looked_up(perm_ref, kbuf[p])
         perm_buf[p] = perm
         w0[p] = c - ADV * perm * c * dbuf[p] - CENTRE * c + BESIDE * nbuf[p]
+
+    def arriving(source, target, send, recv, p):
+        return pltpu.make_async_remote_copy(
+            src_ref=source, dst_ref=target, send_sem=send, recv_sem=recv,
+            device_id={"tm": lax.rem(t + 1, T), "space": p}, device_id_type=pl.DeviceIdType.MESH)
+
+    def jump_copy(p):
+        return arriving(jsrc.at[p], jbuf.at[me], j_send.at[p], j_recv.at[me], p)
+
+    def coarse_copy(p):
+        return arriving(gsrc.at[p], gbuf.at[me], g_send.at[p], g_recv.at[me], p)
+
+    chain_copy = arriving(hsrc, hbuf, h_send.at[0], h_recv.at[0], me)
 
     krylov = (w0, w1, w2, w3)
     for fine in range(FINE):
@@ -242,12 +274,8 @@
         if fine == 0:
             whole = jnp.concatenate([cbuf[p][own] for p in range(S)], axis=0)
             kinds = jnp.concatenate([kbuf[p][own] for p in range(S)], axis=0)
-            ratio = 1.0 / (1.0 + restricted(looked_up(rate_ref, kinds)))
-            q_buf[...] = ratio * restricted(whole)
-        if fine == FINE - 1:
-            from_start = prolonged(q_buf[...])
-            for p in range(S):
-                jsrc[p] = cbuf[p][own] - from_start[p * rows:(p + 1) * rows]
+            ratio_buf[...] = 1.0 / (1.0 + restricted(looked_up(rate_ref, kinds)))
+            rs_buf[...] = restricted(whole)
         for copy in m_copies:
             copy.wait()
         total = mbuf[fine, 0]
@@ -268,77 +296,67 @@
                 w0[p] = c - ADV * perm_buf[p] * c * apart_c - CENTRE * c + BESIDE * near
         else:
             for p in range(S):
-                jsrc[p] += a[0] * w0[p][own] + a[1] * w1[p][own] + a[2] * w2[p][own]
-
-    def jump_copy(p):
-        return pltpu.make_async_remote_copy(
-            src_ref=jsrc.at[p], dst_ref=jbuf.at[me],
-            send_sem=j_send.at[p], recv_sem=j_recv.at[me],
-            device_id={"tm": lax.rem(t + 1, T), "space": p}, device_id_type=pl.DeviceIdType.MESH)
-
-    def coarse_copy(p, ahead):
-        return pltpu.make_async_remote_copy(
-            src_ref=gsrc.at[p], dst_ref=gbuf.at[lax.rem(t, T - 2), me],
-            send_sem=g_send.at[ahead - 2, p], recv_sem=g_recv.at[lax.rem(t, T - 2), me],
-            device_id={"tm": lax.rem(t + ahead, T), "space": p}, device_id_type=pl.DeviceIdType.MESH)
-
-    @pl.when(t < T - 1)
+                jsrc[p] = cbuf[p][own] + (a[0] * w0[p][own] + a[1] * w1[p][own] + a[2] * w2[p][own])
+
+                @pl.when(t < T - 1)
+                def _():
+                    jump_copy(p).start()
+
+    @pl.when(t < T - 2)
+    def _():
+        hsrc[...] = restricted(jsrc[...].reshape(NY, NZ))
+
+    @pl.when((t > 0) & (t < T - 1))
+    def _():
+        chain_copy.wait_recv()
+        correction = ratio_buf[...] * (hbuf[...] - rs_buf[...])
+        gsrc[...] = correction.reshape(S, rows // 2, NZ // 2)
+
+    @pl.when((t > 0) & (t < T - 2))
+    def _():
+        hsrc[...] += gsrc[...].reshape(NY // 2, NZ // 2)
+
+    @pl.when(t < T - 2)
+    def _():
+        chain_copy.start()
+
+    @pl.when((t > 0) & (t < T - 1))
     def _():
         for p in range(S):
-            jump_copy(p).start()
-
-    @pl.when(t < T - 2)
-    def _():
-        jump = jsrc[...].reshape(NY, NZ)
-        gsrc[...] = restricted(jump).reshape(S, rows // 2, NZ // 2)
-        for ahead in range(2, T):
-            @pl.when(t + ahead < T)
-            def _():
-                for p in range(S):
-                    coarse_copy(p, ahead).start()
-
-    @pl.when(t == 0)
-    def _():
-        out_ref[...] = ext[HALO:HALO + NY]
-        for copy in s_copies:
-            copy.wait_send()
+            coarse_copy(p).start()
+
+    @pl.when(t > 1)
+    def _():
+        for p in range(S):
+            arriving(gsrc.at[p], gbuf.at[p], g_send.at[p], g_recv.at[p], p).wait_recv()
+        out_ref[...] = prolonged(gbuf[...].reshape(NY // 2, NZ // 2))
+
+    @pl.when(t == 1)
+    def _():
+        out_ref[...] = jnp.zeros_like(out_ref)
 
     @pl.when(t > 0)
     def _():
-        s_copies[0].wait_recv()
-        for k in range(T - 2):
-            @pl.when(k < t - 1)
-            def _():
-                for p in range(S):
-                    pltpu.make_async_remote_copy(
-                        src_ref=gsrc.at[p], dst_ref=gbuf.at[k, p],
-                        send_sem=g_send.at[0, p], recv_sem=g_recv.at[k, p],
-                        device_id={"tm": lax.rem(t + 1, T), "space": p},
-                        device_id_type=pl.DeviceIdType.MESH).wait_recv()
-                sbuf[...] = out_ratio * sbuf[...] + gbuf[k].reshape(NY // 2, NZ // 2)
-        wide = prolonged(out_ratio * sbuf[...])
         for p in range(S):
-            pltpu.make_async_remote_copy(
-                src_ref=jsrc.at[p], dst_ref=jbuf.at[p],
-                send_sem=j_send.at[p], recv_sem=j_recv.at[p],
-                device_id={"tm": lax.rem(t + 1, T), "space": p},
-                device_id_type=pl.DeviceIdType.MESH).wait_recv()
-        out_ref[...] = wide + jbuf[...].reshape(NY, NZ)
-
-    for copy in c_copies:
-        copy.wait_send()
-    for copy in k_copies:
+            arriving(jsrc.at[p], jbuf.at[p], j_send.at[p], j_recv.at[p], p).wait_recv()
+        out_ref[...] += jbuf[...].reshape(NY, NZ)
+
+    for copy in c_copies + k_copies + f_copies:
         copy.wait_send()
 
     @pl.when(t < T - 1)
     def _():
         for p in range(S):
             jump_copy(p).wait_send()
-    for ahead in range(2, T):
-        @pl.when(t + ahead < T)
-        def _():
-            for p in range(S):
-                coarse_copy(p, ahead).wait_send()
+
+    @pl.when(t < T - 2)
+    def _():
+        chain_copy.wait_send()
+
+    @pl.when((t > 0) & (t < T - 1))
+    def _():
+        for p in range(S):
+            coarse_copy(p).wait_send()
 
 
 def fused_body(S, T, state, classes, perm_table, rate_table):
@@ -346,16 +364,12 @@
     rows = ny // S
     slab = rows + 2 * HALO
     field = pltpu.VMEM((S, slab, nz), F32)
+    coarse = pltpu.VMEM((ny // 2, nz // 2), F32)
     dma = pltpu.SemaphoreType.DMA
     updated = pl.pallas_call(
         functools.partial(kernel, S, T),
         out_shape=jax.ShapeDtypeStruct((ny, nz), F32),
-        in_specs=[
-            pl.BlockSpec(memory_space=pl.ANY),
-            pl.BlockSpec(memory_space=pl.ANY),
-            pl.BlockSpec(memory_space=pltpu.SMEM),
-            pl.BlockSpec(memory_space=pltpu.SMEM),
-        ],
+        in_specs=[pl.BlockSpec(memory_space=pltpu.HBM)] * 4,
         out_specs=pl.BlockSpec(memory_space=pltpu.VMEM),
         scratch_shapes=[
             pltpu.VMEM((ny + 2 * HALO, nz), F32),
@@ -363,22 +377,26 @@
             field,
             pltpu.VMEM((S, slab, nz), jnp.int32),
         ] + [field] * 10 + [
-            pltpu.VMEM((ny // 2, nz // 2), F32),
+            pltpu.SMEM(perm_table.shape, F32),
+            pltpu.SMEM(rate_table.shape, F32),
+            coarse,
+            coarse,
             pltpu.VMEM((FINE, 8, nz // 2), F32),
             pltpu.VMEM((FINE, S, 8, nz // 2), F32),
             pltpu.VMEM((S, rows, nz), F32),
             pltpu.VMEM((S, rows, nz), F32),
             pltpu.VMEM((S, rows // 2, nz // 2), F32),
-            pltpu.VMEM((T - 2, S, rows // 2, nz // 2), F32),
-            pltpu.VMEM((ny // 2, nz // 2), F32),
-            pltpu.VMEM((ny // 2, nz // 2), F32),
-            dma((6,)),
+            pltpu.VMEM((S, rows // 2, nz // 2), F32),
+            coarse,
+            coarse,
+            dma((8,)),
             dma((S - 1,)), dma((S - 1,)),
             dma((S - 1,)), dma((S - 1,)),
+            dma((S - 1, T - 1)), dma((S - 1, T - 1)),
             dma((FINE, S - 1)), dma((FINE, S - 1)),
             dma((S,)), dma((S,)),
-            dma((T - 2, S)), dma((T - 2, S)),
-            dma((T - 1,)), dma((1,)),
+            dma((S,)), dma((S,)),
+            dma((1,)), dma((1,)),
         ],
         compiler_params=pltpu.CompilerParams(
             collective_id=0, has_side_effects=True, vmem_limit_bytes=40 * 1024 * 1024),
@@ -499,7 +517,7 @@
     def chosen(state, classes, perm_table, rate_table):
         planes, ny, nz = state.shape[1:]
         fits = planes == 1 and ny // devices >= 4 * HALO and nz % 256 == 0
-        if fits and slices >= 3 and devices >= 3:
+        if fits and slices == 4 and devices >= 3:
             return fused_body(devices, slices, state, classes, perm_table, rate_table)
         return body(state, classes, perm_table, rate_table)
 

time: 43.8 us -> 38.4 us (0.88)
  Pallas kernels: 40.3 us -> 34.9 us
    pallas_call x1, Pallas kernels: 40.3 us -> 34.9 us  [fused_body(): pl.pallas_call(functools.partial(kernel, S, T), out_shape=jax.ShapeDtypeS...]
where the time goes in v2:
time: 38.4 us; the launch traced here: 38.2 us
  Pallas kernels  34.9 us (91%)
  local copies, waits for them, and re-layouts  3.27 us (9%)
    pallas_call x1, Pallas kernels, fused_body(): pl.pallas_call(functools.partial(kernel, S, T), out_shape=jax.ShapeDtypeS...  34.9 us
    unnamed x9, local copies, waits for them, and re-layouts  3.27 us

profile of v2, /device:TPU:3, one launch (start us, length us, event | category | flops | bytes accessed | tf_op | source)
XLA Modules:
  0.0 38.2 jit_solution(12575201054055050968)
XLA Ops:
  0.0 0.0 copy-start.2
  0.0 0.0 copy-start.3
  0.0 0.7 %copy-done.2 = f32[4]{0:T(128)S(1)} copy-done((f32[4]{0:T(128)S(1)}, f32[4]{0:T(128)}, u32[]{:S(2)}) %copy-start.2) | copy-done | bytes 40
  0.7 0.0 copy-done.3
  0.7 0.0 copy-start
  0.7 0.9 %copy-done = f32[1,1,256,256]{3,2,1,0:T(8,128)S(1)} copy-done((f32[1,1,256,256]{3,2,1,0:T(8,128)S(1)}, f32[1,1,256,256]{3,2,1,0:T(8,128)}, u32[]{:S(2)}) %copy-start) | copy-done | bytes 262168
  1.6 0.0 copy-start.1
  1.6 0.9 %copy-done.1 = s32[1,256,256]{2,1,0:T(8,128)S(1)} copy-done((s32[1,256,256]{2,1,0:T(8,128)S(1)}, s32[1,256,256]{2,1,0:T(8,128)}, u32[]{:S(2)}) %copy-start.1) | copy-done | bytes 262168
  2.6 34.9 %shard_map.46 = f32[256,256]{1,0:T(8,128)S(1)} custom-call(f32[256,256]{1,0:T(8,128)S(1)} %bitcast.4, s32[256,256]{1,0:T(8,128)S(1)} %bitcast.5, f32[4]{0:T(128)S(1)} %copy-done.2, f32[4]{0:T(128)S(1)} %copy-done.3), custom_call_target="tpu_custom_call" | custom-call | tf_op jit(solution)/shard_map/pallas_call | solution.py:369
  37.5 0.7 %copy.6 = f32[1,1,256,256]{3,2,1,0:T(8,128)} copy(f32[1,1,256,256]{3,2,1,0:T(8,128)S(1)} %bitcast.3) | data formatting | bytes 524288
Async XLA Ops:
  0.0 0.7 %copy-start.2 = (f32[4]{0:T(128)S(1)}, f32[4]{0:T(128)}, u32[]{:S(2)}) copy-start(f32[4]{0:T(128)} %perm_hbm.1) | copy-start | bytes 52
  0.0 0.7 %copy-start.3 = (f32[4]{0:T(128)S(1)}, f32[4]{0:T(128)}, u32[]{:S(2)}) copy-start(f32[4]{0:T(128)} %rate_hbm.1) | copy-start | bytes 52
  0.7 0.9 %copy-start = (f32[1,1,256,256]{3,2,1,0:T(8,128)S(1)}, f32[1,1,256,256]{3,2,1,0:T(8,128)}, u32[]{:S(2)}) copy-start(f32[1,1,256,256]{3,2,1,0:T(8,128)} %param.4) | copy-start | bytes 786436
  1.6 0.9 %copy-start.1 = (s32[1,256,256]{2,1,0:T(8,128)S(1)}, s32[1,256,256]{2,1,0:T(8,128)}, u32[]{:S(2)}) copy-start(s32[1,256,256]{2,1,0:T(8,128)} %param.5) | copy-start | bytes 786436

commit v3 on v2

--- a/solution.py
+++ b/solution.py
@@ -399,7 +399,7 @@
             dma((1,)), dma((1,)),
         ],
         compiler_params=pltpu.CompilerParams(
-            collective_id=0, has_side_effects=True, vmem_limit_bytes=40 * 1024 * 1024),
+            collective_id=0, has_side_effects=True, vmem_limit_bytes=56 * 1024 * 1024),
     )(state[0, 0], classes[0], perm_table, rate_table)
     return updated[None, None]
 

time: 38.4 us -> 37.3 us (0.971)
  local copies, waits for them, and re-layouts: 3.27 us -> 1.67 us
  Pallas kernels: 34.9 us -> 35.5 us
    unnamed x9 -> x1, local copies, waits for them, and re-layouts: 3.27 us -> 1.67 us
    pallas_call x1, Pallas kernels: 34.9 us -> 35.5 us  [fused_body(): pl.pallas_call(functools.partial(kernel, S, T), out_shape=jax.ShapeDtypeS...]
where the time goes in v3:
time: 37.3 us; the launch traced here: 37.2 us
  Pallas kernels  35.5 us (95%)
  local copies, waits for them, and re-layouts  1.67 us (4%)
    pallas_call x1, Pallas kernels, fused_body(): pl.pallas_call(functools.partial(kernel, S, T), out_shape=jax.ShapeDtypeS...  35.5 us
    unnamed x1, local copies, waits for them, and re-layouts  1.67 us

profile of v3, /device:TPU:3, one launch (start us, length us, event | category | flops | bytes accessed | tf_op | source)
XLA Modules:
  0.0 37.2 jit_solution(6343149825956480674)
XLA Ops:
  0.0 35.5 %shard_map.46 = f32[256,256]{1,0:T(8,128)} custom-call(f32[256,256]{1,0:T(8,128)} %bitcast.4, s32[256,256]{1,0:T(8,128)} %bitcast.5, f32[4]{0:T(128)} %perm_hbm.1, f32[4]{0:T(128)} %rate_hbm.1), custom_call_target="tpu_custom_call" | custom-call | tf_op jit(solution)/shard_map/pallas_call | solution.py:369
  35.5 1.7 %copy.6 = f32[1,1,256,256]{3,2,1,0:T(8,128)} copy(f32[1,1,256,256]{3,2,1,0:T(8,128)} %bitcast.3) | data formatting | bytes 524288

commit v4 on v3

--- a/solution.py
+++ b/solution.py
@@ -199,16 +199,21 @@
         for e in range(1, T):
             f_copies[(d - 1) * (T - 1) + e - 1].start()
 
-    i = lax.broadcasted_iota(jnp.int32, (NZ, NZ), 0)
-    j = lax.broadcasted_iota(jnp.int32, (NZ, NZ), 1)
-    up, down = i - j == 1, j - i == 1
-    both = jnp.where(up | down, 1.0, 0.0).astype(BF16)
-    apart = jnp.where(up, 1.0, jnp.where(down, -1.0, 0.0)).astype(BF16)
+    lane = lax.broadcasted_iota(jnp.int32, (slab, NZ), 1)
+
+    def vertical_pair(value):
+        upper = jnp.where(lane == NZ - 1, 0.0, pltpu.roll(value, NZ - 1, 1))
+        lower = jnp.where(lane == 0, 0.0, pltpu.roll(value, 1, 1))
+        return upper, lower
+
+    def apart(value):
+        upper, lower = vertical_pair(value)
+        return upper - lower
 
     def neighbours(ref, p):
         value = ref[p]
-        total = times(value, both)
-        total = total + (ref[(p + 1) % S] + ref[(p + S - 1) % S])
+        upper, lower = vertical_pair(value)
+        total = (upper + lower) + (ref[(p + 1) % S] + ref[(p + S - 1) % S])
         total = total + (pltpu.roll(value, 1, 0) + pltpu.roll(value, slab - 1, 0))
         return SCALE * total
 
@@ -220,7 +225,7 @@
         copy.wait_recv()
     for p in range(S):
         nbuf[p] = neighbours(cbuf, p)
-        dbuf[p] = times(cbuf[p], apart)
+        dbuf[p] = apart(cbuf[p])
     for copy in f_copies:
         copy.wait_recv()
     for p in range(S):
@@ -268,9 +273,9 @@
             copy.start()
         if fine < FINE - 1:
             for p in range(S):
-                d0[p] = times(w0[p], apart)
-                d1[p] = times(w1[p], apart)
-                d2[p] = times(w2[p], apart)
+                d0[p] = apart(w0[p])
+                d1[p] = apart(w1[p])
+                d2[p] = apart(w2[p])
         if fine == 0:
             whole = jnp.concatenate([cbuf[p][own] for p in range(S)], axis=0)
             kinds = jnp.concatenate([kbuf[p][own] for p in range(S)], axis=0)

time: 37.3 us -> 36.7 us (0.984)
  Pallas kernels: 35.5 us -> 34.8 us
    pallas_call x1, Pallas kernels: 35.5 us -> 34.8 us  [fused_body(): pl.pallas_call(functools.partial(kernel, S, T), out_shape=jax.ShapeDtypeS...]
where the time goes in v4:
time: 36.7 us; the launch traced here: 36.5 us
  Pallas kernels  34.8 us (95%)
  local copies, waits for them, and re-layouts  1.67 us (5%)
    pallas_call x1, Pallas kernels, fused_body(): pl.pallas_call(functools.partial(kernel, S, T), out_shape=jax.ShapeDtypeS...  34.8 us
    unnamed x1, local copies, waits for them, and re-layouts  1.67 us

profile of v4, /device:TPU:3, one launch (start us, length us, event | category | flops | bytes accessed | tf_op | source)
XLA Modules:
  0.0 36.5 jit_solution(7178917514028997005)
XLA Ops:
  0.0 34.8 %shard_map.46 = f32[256,256]{1,0:T(8,128)} custom-call(f32[256,256]{1,0:T(8,128)} %bitcast.4, s32[256,256]{1,0:T(8,128)} %bitcast.5, f32[4]{0:T(128)} %perm_hbm.1, f32[4]{0:T(128)} %rate_hbm.1), custom_call_target="tpu_custom_call" | custom-call | tf_op jit(solution)/shard_map/pallas_call | solution.py:374
  34.8 1.7 %copy.6 = f32[1,1,256,256]{3,2,1,0:T(8,128)} copy(f32[1,1,256,256]{3,2,1,0:T(8,128)} %bitcast.3) | data formatting | bytes 524288

commit v5 on v4

--- a/solution.py
+++ b/solution.py
@@ -113,7 +113,7 @@
 
 def kernel(S, T, state_ref, classes_ref, perm_hbm, rate_hbm, out_ref,
            ext, extk, cbuf, kbuf, nbuf, dbuf, w0, w1, w2, w3, d0, d1, d2, perm_buf,
-           perm_ref, rate_ref, rs_buf, ratio_buf, msrc, mbuf, jsrc, jbuf, gsrc, gbuf, hsrc, hbuf,
+           perm_ref, rate_ref, rs_buf, ratio_buf, msrc, mbuf, jsrc, jbuf, gsrc, gbuf, hsrc, hbuf, parts_of,
            local_sem, c_send, c_recv, k_send, k_recv, f_send, f_recv, m_send, m_recv,
            j_send, j_recv, g_send, g_recv, h_send, h_recv):
     NY, NZ = state_ref.shape
@@ -245,7 +245,15 @@
     def coarse_copy(p):
         return arriving(gsrc.at[p], gbuf.at[me], g_send.at[p], g_recv.at[me], p)
 
-    chain_copy = arriving(hsrc, hbuf, h_send.at[0], h_recv.at[0], me)
+    def slab_send(source, slot, ahead, send):
+        return pltpu.make_async_remote_copy(
+            src_ref=source, dst_ref=hbuf.at[slot], send_sem=h_send.at[send], recv_sem=h_recv.at[slot],
+            device_id={"tm": lax.rem(t + ahead, T)}, device_id_type=pl.DeviceIdType.MESH)
+
+    near_copy = slab_send(hsrc, 0, 1, 0)
+    far_copy = slab_send(hsrc, 0, 2, 1)
+    next_copy = slab_send(hsrc, 1, 1, 0)
+    start_copy = slab_send(rs_buf, 2, 1, 2)
 
     krylov = (w0, w1, w2, w3)
     for fine in range(FINE):
@@ -281,6 +289,13 @@
             kinds = jnp.concatenate([kbuf[p][own] for p in range(S)], axis=0)
             ratio_buf[...] = 1.0 / (1.0 + restricted(looked_up(rate_ref, kinds)))
             rs_buf[...] = restricted(whole)
+
+            @pl.when(t == 1)
+            def _():
+                start_copy.start()
+        if fine == FINE - 1:
+            for n, ref in enumerate((cbuf, w0, w1, w2)):
+                parts_of[n] = restricted(jnp.concatenate([ref[p][own] for p in range(S)], axis=0))
         for copy in m_copies:
             copy.wait()
         total = mbuf[fine, 0]
@@ -300,6 +315,18 @@
                 dbuf[p] = apart_c
                 w0[p] = c - ADV * perm_buf[p] * c * apart_c - CENTRE * c + BESIDE * near
         else:
+            half = [x[:, :NZ // 2] for x in a]
+            hsrc[...] = parts_of[0] + (half[0] * parts_of[1] + half[1] * parts_of[2] + half[2] * parts_of[3])
+
+            @pl.when(t == 0)
+            def _():
+                far_copy.start()
+                near_copy.start()
+
+            @pl.when(t == 1)
+            def _():
+                next_copy.start()
+
             for p in range(S):
                 jsrc[p] = cbuf[p][own] + (a[0] * w0[p][own] + a[1] * w1[p][own] + a[2] * w2[p][own])
 
@@ -307,23 +334,18 @@
                 def _():
                     jump_copy(p).start()
 
-    @pl.when(t < T - 2)
-    def _():
-        hsrc[...] = restricted(jsrc[...].reshape(NY, NZ))
-
-    @pl.when((t > 0) & (t < T - 1))
-    def _():
-        chain_copy.wait_recv()
-        correction = ratio_buf[...] * (hbuf[...] - rs_buf[...])
-        gsrc[...] = correction.reshape(S, rows // 2, NZ // 2)
-
-    @pl.when((t > 0) & (t < T - 2))
-    def _():
-        hsrc[...] += gsrc[...].reshape(NY // 2, NZ // 2)
-
-    @pl.when(t < T - 2)
-    def _():
-        chain_copy.start()
+    @pl.when(t == 1)
+    def _():
+        near_copy.wait_recv()
+        gsrc[...] = (ratio_buf[...] * (hbuf[0] - rs_buf[...])).reshape(S, rows // 2, NZ // 2)
+
+    @pl.when(t == 2)
+    def _():
+        start_copy.wait_recv()
+        near_copy.wait_recv()
+        first = ratio_buf[...] * (hbuf[0] - hbuf[2]) - rs_buf[...]
+        next_copy.wait_recv()
+        gsrc[...] = (ratio_buf[...] * (first + hbuf[1])).reshape(S, rows // 2, NZ // 2)
 
     @pl.when((t > 0) & (t < T - 1))
     def _():
@@ -354,9 +376,15 @@
         for p in range(S):
             jump_copy(p).wait_send()
 
-    @pl.when(t < T - 2)
-    def _():
-        chain_copy.wait_send()
+    @pl.when(t == 0)
+    def _():
+        far_copy.wait_send()
+        near_copy.wait_send()
+
+    @pl.when(t == 1)
+    def _():
+        next_copy.wait_send()
+        start_copy.wait_send()
 
     @pl.when((t > 0) & (t < T - 1))
     def _():
@@ -393,7 +421,8 @@
             pltpu.VMEM((S, rows // 2, nz // 2), F32),
             pltpu.VMEM((S, rows // 2, nz // 2), F32),
             coarse,
-            coarse,
+            pltpu.VMEM((3, ny // 2, nz // 2), F32),
+            pltpu.VMEM((4, ny // 2, nz // 2), F32),
             dma((8,)),
             dma((S - 1,)), dma((S - 1,)),
             dma((S - 1,)), dma((S - 1,)),
@@ -401,7 +430,7 @@
             dma((FINE, S - 1)), dma((FINE, S - 1)),
             dma((S,)), dma((S,)),
             dma((S,)), dma((S,)),
-            dma((1,)), dma((1,)),
+            dma((3,)), dma((3,)),
         ],
         compiler_params=pltpu.CompilerParams(
             collective_id=0, has_side_effects=True, vmem_limit_bytes=56 * 1024 * 1024),

time: 36.7 us -> 36.8 us (level)
  no operation moved by 1% of the time
where the time goes in v5:
time: 36.8 us; the launch traced here: 36.7 us
  Pallas kernels  35 us (95%)
  local copies, waits for them, and re-layouts  1.67 us (5%)
    pallas_call x1, Pallas kernels, fused_body(): pl.pallas_call(functools.partial(kernel, S, T), out_shape=jax.ShapeDtypeS...  35 us
    unnamed x1, local copies, waits for them, and re-layouts  1.67 us

profile of v5, /device:TPU:3, one launch (start us, length us, event | category | flops | bytes accessed | tf_op | source)
XLA Modules:
  0.0 36.7 jit_solution(4627847915020971163)
XLA Ops:
  0.0 35.0 %shard_map.46 = f32[256,256]{1,0:T(8,128)} custom-call(f32[256,256]{1,0:T(8,128)} %bitcast.4, s32[256,256]{1,0:T(8,128)} %bitcast.5, f32[4]{0:T(128)} %perm_hbm.1, f32[4]{0:T(128)} %rate_hbm.1), custom_call_target="tpu_custom_call" | custom-call | tf_op jit(solution)/shard_map/pallas_call | solution.py:402
  35.0 1.7 %copy.6 = f32[1,1,256,256]{3,2,1,0:T(8,128)} copy(f32[1,1,256,256]{3,2,1,0:T(8,128)} %bitcast.3) | data formatting | bytes 524288

commit v6 on v5

--- a/solution.py
+++ b/solution.py
@@ -113,9 +113,9 @@
 
 def kernel(S, T, state_ref, classes_ref, perm_hbm, rate_hbm, out_ref,
            ext, extk, cbuf, kbuf, nbuf, dbuf, w0, w1, w2, w3, d0, d1, d2, perm_buf,
-           perm_ref, rate_ref, rs_buf, ratio_buf, msrc, mbuf, jsrc, jbuf, gsrc, gbuf, hsrc, hbuf, parts_of,
+           perm_ref, rate_ref, rs_buf, ratio_buf, msrc, mbuf, jsrc, jbuf, gbuf, hsrc, sbuf, parts_of,
            local_sem, c_send, c_recv, k_send, k_recv, f_send, f_recv, m_send, m_recv,
-           j_send, j_recv, g_send, g_recv, h_send, h_recv):
+           j_send, j_recv, g_send, g_recv, s_send, s_recv):
     NY, NZ = state_ref.shape
     rows = NY // S
     slab = rows + 2 * HALO
@@ -140,7 +140,7 @@
         copy.start()
 
     barrier = pltpu.get_barrier_semaphore()
-    partners = [(dt, dz) for dt in range(T) for dz in range(S) if dz == 0 or dt in (0, 1, T - 1)][1:]
+    partners = [(dt, dz) for dt in range(T) for dz in range(S)][1:]
     for dt, dz in partners:
         pl.semaphore_signal(
             barrier, inc=1,
@@ -190,9 +190,26 @@
     cbuf[me] = ext[mine]
     kbuf[me] = extk[mine]
 
+    def start_send(slot, ahead):
+        return pltpu.make_async_remote_copy(
+            src_ref=rs_buf, dst_ref=sbuf.at[slot], send_sem=s_send.at[ahead - 1], recv_sem=s_recv.at[slot],
+            device_id={"tm": lax.rem(t + ahead, T)}, device_id_type=pl.DeviceIdType.MESH)
+
+    first_near, first_far, second_near = start_send(0, 1), start_send(0, 2), start_send(1, 1)
+    rs_buf[...] = restricted(ext[HALO:HALO + NY])
+
     @pl.when(t == 0)
     def _():
         out_ref[...] = ext[HALO:HALO + NY]
+
+    @pl.when(t == 1)
+    def _():
+        first_near.start()
+        first_far.start()
+
+    @pl.when(t == 2)
+    def _():
+        second_near.start()
 
     for d in range(1, S):
         k_copies[d - 1].wait_recv()
@@ -242,18 +259,11 @@
     def jump_copy(p):
         return arriving(jsrc.at[p], jbuf.at[me], j_send.at[p], j_recv.at[me], p)
 
-    def coarse_copy(p):
-        return arriving(gsrc.at[p], gbuf.at[me], g_send.at[p], g_recv.at[me], p)
-
-    def slab_send(source, slot, ahead, send):
+    def coarse_copy(p, slot, ahead):
         return pltpu.make_async_remote_copy(
-            src_ref=source, dst_ref=hbuf.at[slot], send_sem=h_send.at[send], recv_sem=h_recv.at[slot],
-            device_id={"tm": lax.rem(t + ahead, T)}, device_id_type=pl.DeviceIdType.MESH)
-
-    near_copy = slab_send(hsrc, 0, 1, 0)
-    far_copy = slab_send(hsrc, 0, 2, 1)
-    next_copy = slab_send(hsrc, 1, 1, 0)
-    start_copy = slab_send(rs_buf, 2, 1, 2)
+            src_ref=hsrc.at[p], dst_ref=gbuf.at[slot, me],
+            send_sem=g_send.at[ahead - 2, p], recv_sem=g_recv.at[slot, me],
+            device_id={"tm": lax.rem(t + ahead, T), "space": p}, device_id_type=pl.DeviceIdType.MESH)
 
     krylov = (w0, w1, w2, w3)
     for fine in range(FINE):
@@ -285,14 +295,7 @@
                 d1[p] = apart(w1[p])
                 d2[p] = apart(w2[p])
         if fine == 0:
-            whole = jnp.concatenate([cbuf[p][own] for p in range(S)], axis=0)
-            kinds = jnp.concatenate([kbuf[p][own] for p in range(S)], axis=0)
-            ratio_buf[...] = 1.0 / (1.0 + restricted(looked_up(rate_ref, kinds)))
-            rs_buf[...] = restricted(whole)
-
-            @pl.when(t == 1)
-            def _():
-                start_copy.start()
+            ratio_buf[...] = 1.0 / (1.0 + restricted(looked_up(rate_ref, extk[HALO:HALO + NY])))
         if fine == FINE - 1:
             for n, ref in enumerate((cbuf, w0, w1, w2)):
                 parts_of[n] = restricted(jnp.concatenate([ref[p][own] for p in range(S)], axis=0))
@@ -316,16 +319,19 @@
                 w0[p] = c - ADV * perm_buf[p] * c * apart_c - CENTRE * c + BESIDE * near
         else:
             half = [x[:, :NZ // 2] for x in a]
-            hsrc[...] = parts_of[0] + (half[0] * parts_of[1] + half[1] * parts_of[2] + half[2] * parts_of[3])
+            ends = parts_of[0] + (half[0] * parts_of[1] + half[1] * parts_of[2] + half[2] * parts_of[3])
+            hsrc[...] = ends.reshape(S, rows // 2, NZ // 2)
 
             @pl.when(t == 0)
             def _():
-                far_copy.start()
-                near_copy.start()
+                for p in range(S):
+                    coarse_copy(p, 0, 3).start()
+                    coarse_copy(p, 0, 2).start()
 
             @pl.when(t == 1)
             def _():
-                next_copy.start()
+                for p in range(S):
+                    coarse_copy(p, 1, 2).start()
 
             for p in range(S):
                 jsrc[p] = cbuf[p][own] + (a[0] * w0[p][own] + a[1] * w1[p][own] + a[2] * w2[p][own])
@@ -334,29 +340,23 @@
                 def _():
                     jump_copy(p).start()
 
-    @pl.when(t == 1)
-    def _():
-        near_copy.wait_recv()
-        gsrc[...] = (ratio_buf[...] * (hbuf[0] - rs_buf[...])).reshape(S, rows // 2, NZ // 2)
+    def coarse_end(slot):
+        for p in range(S):
+            arriving(hsrc.at[p], gbuf.at[slot, p], g_send.at[0, p], g_recv.at[slot, p], p).wait_recv()
+        return gbuf[slot].reshape(NY // 2, NZ // 2)
 
     @pl.when(t == 2)
     def _():
-        start_copy.wait_recv()
-        near_copy.wait_recv()
-        first = ratio_buf[...] * (hbuf[0] - hbuf[2]) - rs_buf[...]
-        next_copy.wait_recv()
-        gsrc[...] = (ratio_buf[...] * (first + hbuf[1])).reshape(S, rows // 2, NZ // 2)
-
-    @pl.when((t > 0) & (t < T - 1))
-    def _():
-        for p in range(S):
-            coarse_copy(p).start()
-
-    @pl.when(t > 1)
-    def _():
-        for p in range(S):
-            arriving(gsrc.at[p], gbuf.at[p], g_send.at[p], g_recv.at[p], p).wait_recv()
-        out_ref[...] = prolonged(gbuf[...].reshape(NY // 2, NZ // 2))
+        first_near.wait_recv()
+        out_ref[...] = prolonged(ratio_buf[...] * (coarse_end(0) - sbuf[0]))
+
+    @pl.when(t == 3)
+    def _():
+        first_near.wait_recv()
+        second_near.wait_recv()
+        ratio = ratio_buf[...]
+        second = ratio * (coarse_end(0) - sbuf[0]) + (coarse_end(1) - sbuf[1])
+        out_ref[...] = prolonged(ratio * second)
 
     @pl.when(t == 1)
     def _():
@@ -378,18 +378,20 @@
 
     @pl.when(t == 0)
     def _():
-        far_copy.wait_send()
-        near_copy.wait_send()
+        for p in range(S):
+            coarse_copy(p, 0, 3).wait_send()
+            coarse_copy(p, 0, 2).wait_send()
 
     @pl.when(t == 1)
     def _():
-        next_copy.wait_send()
-        start_copy.wait_send()
-
-    @pl.when((t > 0) & (t < T - 1))
-    def _():
+        first_near.wait_send()
+        first_far.wait_send()
         for p in range(S):
-            coarse_copy(p).wait_send()
+            coarse_copy(p, 1, 2).wait_send()
+
+    @pl.when(t == 2)
+    def _():
+        second_near.wait_send()
 
 
 def fused_body(S, T, state, classes, perm_table, rate_table):
@@ -418,10 +420,9 @@
             pltpu.VMEM((FINE, S, 8, nz // 2), F32),
             pltpu.VMEM((S, rows, nz), F32),
             pltpu.VMEM((S, rows, nz), F32),
+            pltpu.VMEM((2, S, rows // 2, nz // 2), F32),
             pltpu.VMEM((S, rows // 2, nz // 2), F32),
-            pltpu.VMEM((S, rows // 2, nz // 2), F32),
-            coarse,
-            pltpu.VMEM((3, ny // 2, nz // 2), F32),
+            pltpu.VMEM((2, ny // 2, nz // 2), F32),
             pltpu.VMEM((4, ny // 2, nz // 2), F32),
             dma((8,)),
             dma((S - 1,)), dma((S - 1,)),
@@ -429,8 +430,8 @@
             dma((S - 1, T - 1)), dma((S - 1, T - 1)),
             dma((FINE, S - 1)), dma((FINE, S - 1)),
             dma((S,)), dma((S,)),
-            dma((S,)), dma((S,)),
-            dma((3,)), dma((3,)),
+            dma((2, S)), dma((2, S)),
+            dma((2,)), dma((2,)),
         ],
         compiler_params=pltpu.CompilerParams(
             collective_id=0, has_side_effects=True, vmem_limit_bytes=56 * 1024 * 1024),

time: 36.8 us -> 35.9 us (0.976)
  the two profiles are of different devices: /device:TPU:3 before, /device:TPU:1 now
where the time goes in v6:
time: 35.9 us; the launch traced here: 35.7 us
  Pallas kernels  34.1 us (95%)
  local copies, waits for them, and re-layouts  1.67 us (5%)
    pallas_call x1, Pallas kernels, fused_body(): pl.pallas_call(functools.partial(kernel, S, T), out_shape=jax.ShapeDtypeS...  34.1 us
    unnamed x1, local copies, waits for them, and re-layouts  1.67 us

profile of v6, /device:TPU:1, one launch (start us, length us, event | category | flops | bytes accessed | tf_op | source)
XLA Modules:
  0.0 35.7 jit_solution(14833244858423384649)
XLA Ops:
  0.0 34.1 %shard_map.46 = f32[256,256]{1,0:T(8,128)} custom-call(f32[256,256]{1,0:T(8,128)} %bitcast.4, s32[256,256]{1,0:T(8,128)} %bitcast.5, f32[4]{0:T(128)} %perm_hbm.1, f32[4]{0:T(128)} %rate_hbm.1), custom_call_target="tpu_custom_call" | custom-call | tf_op jit(solution)/shard_map/pallas_call | solution.py:404
  34.1 1.7 %copy.6 = f32[1,1,256,256]{3,2,1,0:T(8,128)} copy(f32[1,1,256,256]{3,2,1,0:T(8,128)} %bitcast.3) | data formatting | bytes 524288

commit v7 on v6

--- a/solution.py
+++ b/solution.py
@@ -15,8 +15,7 @@
 ADV = 0.25
 
 CENTRE = 1.0 + 6.0 * DIFF
-SCALE = 0.125
-BESIDE = DIFF / SCALE
+BESIDE = DIFF
 LOWEST = CENTRE - 6.0 * DIFF
 HIGHEST = CENTRE + 6.0 * DIFF
 HALO = 8
@@ -216,12 +215,16 @@
         for e in range(1, T):
             f_copies[(d - 1) * (T - 1) + e - 1].start()
 
-    lane = lax.broadcasted_iota(jnp.int32, (slab, NZ), 1)
+    lane = lax.broadcasted_iota(jnp.int32, (slab, wide), 1)
 
     def vertical_pair(value):
-        upper = jnp.where(lane == NZ - 1, 0.0, pltpu.roll(value, NZ - 1, 1))
-        lower = jnp.where(lane == 0, 0.0, pltpu.roll(value, 1, 1))
-        return upper, lower
+        low, top = value[:, :wide], value[:, wide:]
+        low_up, top_up = pltpu.roll(low, wide - 1, 1), pltpu.roll(top, wide - 1, 1)
+        low_down, top_down = pltpu.roll(low, 1, 1), pltpu.roll(top, 1, 1)
+        last, first = lane == wide - 1, lane == 0
+        upper = (jnp.where(last, top_up, low_up), jnp.where(last, 0.0, top_up))
+        lower = (jnp.where(first, 0.0, low_down), jnp.where(first, low_down, top_down))
+        return jnp.concatenate(upper, axis=1), jnp.concatenate(lower, axis=1)
 
     def apart(value):
         upper, lower = vertical_pair(value)
@@ -232,7 +235,7 @@
         upper, lower = vertical_pair(value)
         total = (upper + lower) + (ref[(p + 1) % S] + ref[(p + S - 1) % S])
         total = total + (pltpu.roll(value, 1, 0) + pltpu.roll(value, slab - 1, 0))
-        return SCALE * total
+        return total
 
     def dot_rows(a, b):
         product = (a * b)[own]
@@ -551,7 +554,7 @@
 
     def chosen(state, classes, perm_table, rate_table):
         planes, ny, nz = state.shape[1:]
-        fits = planes == 1 and ny // devices >= 4 * HALO and nz % 256 == 0
+        fits = planes == 1 and ny // devices >= 4 * HALO and nz == 256
         if fits and slices == 4 and devices >= 3:
             return fused_body(devices, slices, state, classes, perm_table, rate_table)
         return body(state, classes, perm_table, rate_table)

time: 35.9 us -> 35.7 us (level)
  no operation moved by 1% of the time
where the time goes in v7:
time: 35.7 us; the launch traced here: 35.6 us
  Pallas kernels  33.9 us (95%)
  local copies, waits for them, and re-layouts  1.67 us (5%)
    pallas_call x1, Pallas kernels, fused_body(): pl.pallas_call(functools.partial(kernel, S, T), out_shape=jax.ShapeDtypeS...  33.9 us
    unnamed x1, local copies, waits for them, and re-layouts  1.67 us

profile of v7, /device:TPU:1, one launch (start us, length us, event | category | flops | bytes accessed | tf_op | source)
XLA Modules:
  0.0 35.6 jit_solution(12982589797245792775)
XLA Ops:
  0.0 33.9 %shard_map.46 = f32[256,256]{1,0:T(8,128)} custom-call(f32[256,256]{1,0:T(8,128)} %bitcast.4, s32[256,256]{1,0:T(8,128)} %bitcast.5, f32[4]{0:T(128)} %perm_hbm.1, f32[4]{0:T(128)} %rate_hbm.1), custom_call_target="tpu_custom_call" | custom-call | tf_op jit(solution)/shard_map/pallas_call | solution.py:407
  33.9 1.7 %copy.6 = f32[1,1,256,256]{3,2,1,0:T(8,128)} copy(f32[1,1,256,256]{3,2,1,0:T(8,128)} %bitcast.3) | data formatting | bytes 524288
